TPU v7x, 256 devices: a whole 4x4x8 slice. The times are simulated.
256 devices in a mesh: bx: 2 (over core), by: 4 (over z_lo), bz: 32 (over z_hi, y, x).
Axes of the slice: x: 4, y: 4, z: 8 (z_hi: 2, z_lo: 4; z = z_hi * 4 + z_lo), core: 2. Of those that a mesh axis runs over, the one named last changes fastest.
Arguments:
- skel_blocks: bfloat16 [2, 4, 32, 2, 256, 256], P('bx', 'by', 'bz'), may hold values from -6 to 6
- row_couple: bfloat16 [2, 4, 32, 27, 256, 256], P('bx', 'by', 'bz'), may hold values from -0.375 to 0.375
- col_couple: bfloat16 [2, 4, 32, 27, 256, 256], P('bx', 'by', 'bz'), may hold values from -0.375 to 0.375
- inverse_rr: bfloat16 [2, 4, 32, 256, 256], P('bx', 'by', 'bz'), may hold values from -0.0048828125 to 0.0048828125
- pivots: int32 [2, 4, 32, 256], P('bx', 'by', 'bz'), may hold values from 0 to 255, each once within a row
- self_block: float32 [2, 4, 32, 256, 256], P('bx', 'by', 'bz'), may hold values from -6 to 6
- skel_count: int32 [2, 4, 32], P('bx', 'by', 'bz'), may hold values from 64 to 256
- skel_order: int32 [2, 4, 32, 256], P('bx', 'by', 'bz'), may hold values from 0 to 255, each once within a row
- owner_flag: int32 [2, 4, 16], P('bx', 'by'), may hold values 0 or 1
Outputs:
- updated_self: float32 [2, 4, 32, 256, 256], P('bx', 'by', 'bz')
- parent_blocks: float32 [2, 4, 32, 2, 256, 256], P('bx', 'by', 'bz')
Inputs may be any that keep to these rules, and one draw needn't show every extreme that they name: Each box's pivots are a permutation of 0 to 255. `skel_order`: each box's skeleton index list is a permutation of 0 to 255.
All inputs are finite; a program needn't handle non-finite values. No bound on the sum of `owner_flag` on one device may be relied on, other than what follows from the above.
Results may differ from a plain program's by a relative error of at most 0.0027.
Values may be sent and summed in bfloat16 or wider, within the bound.
No kernel may reach another device: no remote copies, remote signals or barrier semaphores. Data moves between devices by JAX's collectives and lax.ppermute only.
A program may use at most 64 MiB of HBM per device.

v0:
```python
import jax
import jax.numpy as jnp
from jax import lax
from jax.sharding import PartitionSpec as P


def shifted(block, axis, distance):
    devices = range(lax.axis_size(axis))
    route = [(i - distance, i) for i in devices if i - distance in devices]
    return lax.ppermute(block, axis, route)


def padded(cells, sides, width):
    for axis, dim in sides:
        count = lax.axis_size(axis)
        ends = count - 1
        head = lax.slice_in_dim(cells, 0, width, axis=dim)
        tail = lax.slice_in_dim(cells, cells.shape[dim] - width, cells.shape[dim], axis=dim)
        cells = jnp.concatenate(
            [
                lax.ppermute(tail, axis, [(i, (i + 1) % count) for i in range(ends)]),
                cells,
                lax.ppermute(head, axis, [((i + 1) % count, i) for i in range(ends)]),
            ],
            axis=dim,
        )
    return cells


def swapped(block, axis, distance):
    count = lax.axis_size(axis)
    route = []
    for low in range(count):
        high = low | 1 << distance
        if high != low and high < count:
            route += [(low, high), (high, low)]
    return lax.ppermute(block, axis, route)


def move_along_x(lower_part, middle, upper_part):
    return (shifted(lower_part, "bx", -1), middle, shifted(upper_part, "bx", 1))


def move_along_y(lower_part, middle, upper_part):
    return (shifted(lower_part, "by", -1), middle, shifted(upper_part, "by", 1))


def move_along_z(lower_part, middle, upper_part):
    return (shifted(lower_part, "bz", -1), middle, shifted(upper_part, "bz", 1))


def on_device(
    skel_blocks,
    row_couple,
    col_couple,
    inverse_rr,
    pivots,
    self_block,
    skel_count,
    skel_order,
    owner_flag,
):
    size_s = skel_blocks.shape[4]
    points = lax.iota(jnp.int32, size_s)
    count = skel_count[0, 0, 0]
    live = (points < count).astype(jnp.bfloat16)
    masked = skel_blocks * live[None, None, None, None, :, None]
    nearby = padded(masked, (("bx", 0), ("by", 1), ("bz", 2)), 1)
    nearby = nearby.reshape(27, 2, size_s, skel_blocks.shape[5])
    upper = jnp.einsum(
        "osq,oqr->osr", nearby[:, 0], row_couple[0, 0, 0], preferred_element_type=jnp.float32
    ).astype(jnp.bfloat16)
    lower = jnp.einsum(
        "orq,osq->ors", col_couple[0, 0, 0], nearby[:, 1], preferred_element_type=jnp.float32
    ).astype(jnp.bfloat16)
    permuted = lower[:, pivots[0, 0, 0], :]
    solved = jnp.einsum(
        "rk,oks->ors", inverse_rr[0, 0, 0], permuted, preferred_element_type=jnp.float32
    ).astype(jnp.bfloat16)
    contrib = jnp.einsum("osr,ort->ost", upper, solved, preferred_element_type=jnp.float32)
    cube = contrib.reshape(3, 3, 3, size_s, size_s)
    along_x = jnp.stack(move_along_x(cube[0], cube[1], cube[2]), axis=0)
    along_y = jnp.stack(move_along_y(along_x[:, 0], along_x[:, 1], along_x[:, 2]), axis=1)
    along_z = jnp.stack(move_along_z(along_y[:, :, 0], along_y[:, :, 1], along_y[:, :, 2]), axis=2)
    total = jnp.sum(along_z, axis=(0, 1, 2))
    updated = self_block[0, 0, 0] - total
    order = skel_order[0, 0, 0]
    chosen = updated[order][:, order]
    keep = (points[:, None] < count) & (points[None, :] < count)
    child = jnp.where(keep, chosen, jnp.float32(0.0))
    partner = swapped(child, "bz", 0)
    zpos = lax.axis_index("bz")
    parity = zpos % 2
    flag = lax.dynamic_index_in_dim(owner_flag[0, 0], zpos // 2, 0, keepdims=False)
    first = jnp.where(parity == 0, child, partner)
    second = jnp.where(parity == 0, partner, child)
    stacked = jnp.stack((first, second), axis=0)
    parent = jnp.where(parity == flag, stacked, jnp.float32(0.0))
    return (updated[None, None, None], parent[None, None, None])


def solution(mesh):
    in_specs = (
        P("bx", "by", "bz", None, None, None),
        P("bx", "by", "bz", None, None, None),
        P("bx", "by", "bz", None, None, None),
        P("bx", "by", "bz", None, None),
        P("bx", "by", "bz", None),
        P("bx", "by", "bz", None, None),
        P("bx", "by", "bz"),
        P("bx", "by", "bz", None),
        P("bx", "by", None),
    )
    out_specs = (P("bx", "by", "bz", None, None), P("bx", "by", "bz", None, None, None))
    return jax.shard_map(
        on_device, mesh=mesh, in_specs=in_specs, out_specs=out_specs, check_vma=False
    )
```

profile of v0, /device:TPU:62, one launch (start us, length us, event | category | flops | bytes accessed | tf_op | source)
XLA Modules:
  0.0 395.0 jit_solution(11422701091651729056)
XLA Ops:
  4.0 3.1 collective-permute-start
  8.3 2.0 collective-permute-start.3
  10.3 3.8 collective-permute-start.2
  14.2 16.0 %collective-permute-done.3 = bf16[3,1,1,2,256,256]{5,4,3,2,1,0:T(8,128)(2,1)S(1)} collective-permute-done((bf16[3,1,1,2,256,256]{5,4,3,2,1,0:T(8,128)(2,1)S(1)}, bf16[3,1,1,2,256,256]{5,4,3,2,1,0:T(8,128)(2,1)S(1)}, u32[]{:S(2)}, u32[]{:S(2)}) %collective-permute-start.3) | collective-permute-done | bytes 786464 | tf_op jit(solution)/shard_map/ppermute | solution.py:23
  32.3 2.7 collective-permute-start.5
  35.0 11.2 %collective-permute-start.4 = (bf16[3,3,1,2,256,256]{5,4,3,2,1,0:T(8,128)(2,1)S(1)}, bf16[3,3,1,2,256,256]{5,4,3,2,1,0:T(8,128)(2,1)S(1)}, u32[]{:S(2)}, u32[]{:S(2)}) collective-permute-start(bf16[3,3,1,2,256,256]{5,4,3,2,1,0:T(8,128)(2,1)S(1)} %pad_maximum_fusion.3), channel_id=1, source_target_pairs={{0,1},{1,2},{2,3},{3,4},{4,5},{5,6},{6,7},{7,8},{8,9},{9,10},{10,1... | collective-permute-start | bytes 7077896 | tf_op jit(solution)/shard_map/ppermute | solution.py:21
  46.3 99.3 %collective-permute-done.5 = bf16[3,3,1,2,256,256]{5,4,3,2,1,0:T(8,128)(2,1)S(1)} collective-permute-done((bf16[3,3,1,2,256,256]{5,4,3,2,1,0:T(8,128)(2,1)S(1)}, bf16[3,3,1,2,256,256]{5,4,3,2,1,0:T(8,128)(2,1)S(1)}, u32[]{:S(2)}, u32[]{:S(2)}) %collective-permute-start.5) | collective-permute-done | bytes 2359328 | tf_op jit(solution)/shard_map/ppermute | solution.py:23
  147.5 2.9 fusion.1
  151.5 6.1 %copy.19 = bf16[27,256,256]{1,0,2:T(8,128)(2,1)} copy(bf16[27,256,256]{2,1,0:T(8,128)(2,1)S(1)} %fusion) | data formatting | bytes 7077888 | tf_op jit(solution)/shard_map/orq,osq->ors/dot_general | solution.py:73
  157.6 5.1 %gather_fusion = bf16[256,27,256]{2,1,0:T(8,128)(2,1)} fusion(bf16[27,256,256]{2,0,1:T(8,128)(2,1)} %bitcast.67, s32[1024]{0:T(1024)S(1)} %pad_clamp_fusion.1), kind=kCustom, calls=%fused_computation | custom fusion | bytes 7078912 | tf_op jit(solution)/shard_map/gather | solution.py:76
  162.7 13.1 %fusion.6 = f32[27,256,256]{2,1,0:T(8,128)} fusion(bf16[27,256,256]{2,1,0:T(8,128)(2,1)S(1)} %copy-done.2, bf16[27,256,256]{2,0,1:T(8,128)(2,1)} %bitcast.68, bf16[1,1,1,256,256]{4,3,2,1,0:T(8,128)(2,1)} %param.12), kind=kOutput, calls=%fused_computation.15 | convolution fusion | flops 1813708800 | bytes 14286848 | tf_op jit(solution)/shard_map/osr,ort->ost/dot_general | solution.py:80
  175.8 3.5 fusion.16
  182.3 2.5 collective-permute-done.7
  184.8 2.4 collective-permute-done.6
  188.5 3.0 collective-permute-start.9
  191.5 3.0 collective-permute-start.8
  194.5 49.2 %collective-permute-done.9 = f32[3,3,256,256]{3,2,1,0:T(8,128)S(1)} collective-permute-done((f32[3,3,256,256]{3,2,1,0:T(8,128)S(1)}, f32[3,3,256,256]{3,2,1,0:T(8,128)S(1)}, u32[]{:S(2)}, u32[]{:S(2)}) %collective-permute-start.9) | collective-permute-done | bytes 2359328 | tf_op jit(solution)/shard_map/ppermute | solution.py:10
  243.7 2.7 collective-permute-done.8
  248.9 12.5 %collective-permute-start.11 = (f32[3,3,256,256]{3,2,0,1:T(8,128)S(1)}, f32[3,3,256,256]{3,2,0,1:T(8,128)}, u32[]{:S(2)}, u32[]{:S(2)}) collective-permute-start(f32[3,3,256,256]{3,2,0,1:T(8,128)S(1)} %get-tuple-element.7), channel_id=1, source_target_pairs={{0,1},{1,2},{2,3},{3,4},{4,5},{5,6},{6,7},{7,8},{8,9},{9,10},{10,1... | collective-permute-start | bytes 7077896 | tf_op jit(solution)/shard_map/ppermute | solution.py:10
  263.4 97.3 %collective-permute-done.11 = f32[3,3,256,256]{3,2,0,1:T(8,128)} collective-permute-done((f32[3,3,256,256]{3,2,0,1:T(8,128)S(1)}, f32[3,3,256,256]{3,2,0,1:T(8,128)}, u32[]{:S(2)}, u32[]{:S(2)}) %collective-permute-start.11) | collective-permute-done | bytes 2359328 | tf_op jit(solution)/shard_map/ppermute | solution.py:10
  362.5 10.6 %collective-permute-done.10 = f32[3,3,256,256]{3,2,0,1:T(8,128)S(1)} collective-permute-done((f32[3,3,256,256]{3,2,0,1:T(8,128)}, f32[3,3,256,256]{3,2,0,1:T(8,128)S(1)}, u32[]{:S(2)}, u32[]{:S(2)}) %collective-permute-start.10) | collective-permute-done | bytes 2359328 | tf_op jit(solution)/shard_map/ppermute | solution.py:10
  378.0 2.6 gather_fusion.2
  385.5 5.4 %collective-permute-done.12 = f32[256,256]{0,1:T(8,128)} collective-permute-done((f32[256,256]{0,1:T(8,128)}, f32[256,256]{0,1:T(8,128)}, u32[]{:S(2)}, u32[]{:S(2)}) %collective-permute-start.12) | collective-permute-done | bytes 262176 | tf_op jit(solution)/shard_map/ppermute | solution.py:37
  392.9 2.0 copy.18
  (54 shorter events, 30.4 us)
Async XLA Ops:
  0.6 146.9 %copy-start = (bf16[1,1,1,27,256,256]{5,4,3,2,1,0:T(8,128)(2,1)S(1)}, bf16[1,1,1,27,256,256]{5,4,3,2,1,0:T(8,128)(2,1)}, u32[]{:S(2)}) copy-start(bf16[1,1,1,27,256,256]{5,4,3,2,1,0:T(8,128)(2,1)} %param.10) | copy-start | bytes 10616836
  0.6 45.6 %copy-start.7 = (s32[1,1,1,256]{3,2,1,0:T(1,128)S(1)}, s32[1,1,1,256]{3,2,1,0:T(1,128)}, u32[]{:S(2)}) copy-start(s32[1,1,1,256]{3,2,1,0:T(1,128)} %param.13) | copy-start | bytes 3076
  2.7 4.4 %collective-permute-start.1 = (bf16[1,1,1,2,256,256]{5,4,3,2,1,0:T(8,128)(2,1)S(1)}, bf16[1,1,1,2,256,256]{5,4,3,2,1,0:T(8,128)(2,1)S(1)}, u32[]{:S(2)}, u32[]{:S(2)}) collective-permute-start(bf16[1,1,1,2,256,256]{5,4,3,2,1,0:T(8,128)(2,1)S(1)} %broadcast_multiply_fusion), channel_id=1, source_target_pairs={{128,0},{129,1},{130,2},{131,3},{132,4},{133,5},{134,6},{135,7},{1... | collective-permute-start | bytes 786440 | tf_op jit(solution)/shard_map/ppermute | solution.py:23
  4.0 4.2 %collective-permute-start = (bf16[1,1,1,2,256,256]{5,4,3,2,1,0:T(8,128)(2,1)S(1)}, bf16[1,1,1,2,256,256]{5,4,3,2,1,0:T(8,128)(2,1)S(1)}, u32[]{:S(2)}, u32[]{:S(2)}) collective-permute-start(bf16[1,1,1,2,256,256]{5,4,3,2,1,0:T(8,128)(2,1)S(1)} %broadcast_multiply_fusion), channel_id=1, source_target_pairs={{0,128},{1,129},{2,130},{3,131},{4,132},{5,133},{6,134},{7,135},{8... | collective-permute-start | bytes 786440 | tf_op jit(solution)/shard_map/ppermute | solution.py:21
  8.3 21.9 %collective-permute-start.3 = (bf16[3,1,1,2,256,256]{5,4,3,2,1,0:T(8,128)(2,1)S(1)}, bf16[3,1,1,2,256,256]{5,4,3,2,1,0:T(8,128)(2,1)S(1)}, u32[]{:S(2)}, u32[]{:S(2)}) collective-permute-start(bf16[3,1,1,2,256,256]{5,4,3,2,1,0:T(8,128)(2,1)S(1)} %pad_maximum_fusion.4), channel_id=1, source_target_pairs={{32,0},{64,32},{96,64},{33,1},{65,33},{97,65},{34,2},{66,34},{98,6... | collective-permute-start | bytes 2359304 | tf_op jit(solution)/shard_map/ppermute | solution.py:23
  10.3 21.6 %collective-permute-start.2 = (bf16[3,1,1,2,256,256]{5,4,3,2,1,0:T(8,128)(2,1)S(1)}, bf16[3,1,1,2,256,256]{5,4,3,2,1,0:T(8,128)(2,1)S(1)}, u32[]{:S(2)}, u32[]{:S(2)}) collective-permute-start(bf16[3,1,1,2,256,256]{5,4,3,2,1,0:T(8,128)(2,1)S(1)} %pad_maximum_fusion.4), channel_id=1, source_target_pairs={{0,32},{32,64},{64,96},{1,33},{33,65},{65,97},{2,34},{34,66},{66,9... | collective-permute-start | bytes 2359304 | tf_op jit(solution)/shard_map/ppermute | solution.py:21
  32.3 113.3 %collective-permute-start.5 = (bf16[3,3,1,2,256,256]{5,4,3,2,1,0:T(8,128)(2,1)S(1)}, bf16[3,3,1,2,256,256]{5,4,3,2,1,0:T(8,128)(2,1)S(1)}, u32[]{:S(2)}, u32[]{:S(2)}) collective-permute-start(bf16[3,3,1,2,256,256]{5,4,3,2,1,0:T(8,128)(2,1)S(1)} %pad_maximum_fusion.3), channel_id=1, source_target_pairs={{1,0},{2,1},{3,2},{4,3},{5,4},{6,5},{7,6},{8,7},{9,8},{10,9},{11,1... | collective-permute-start | bytes 7077896 | tf_op jit(solution)/shard_map/ppermute | solution.py:23
  35.0 111.6 %collective-permute-start.4 = (bf16[3,3,1,2,256,256]{5,4,3,2,1,0:T(8,128)(2,1)S(1)}, bf16[3,3,1,2,256,256]{5,4,3,2,1,0:T(8,128)(2,1)S(1)}, u32[]{:S(2)}, u32[]{:S(2)}) collective-permute-start(bf16[3,3,1,2,256,256]{5,4,3,2,1,0:T(8,128)(2,1)S(1)} %pad_maximum_fusion.3), channel_id=1, source_target_pairs={{0,1},{1,2},{2,3},{3,4},{4,5},{5,6},{6,7},{7,8},{8,9},{9,10},{10,1... | collective-permute-start | bytes 7077896 | tf_op jit(solution)/shard_map/ppermute | solution.py:21
  147.5 2.9 copy-start.3
  157.6 5.1 %copy-start.2 = (bf16[27,256,256]{2,1,0:T(8,128)(2,1)S(1)}, bf16[27,256,256]{2,1,0:T(8,128)(2,1)}, u32[]{:S(2)}) copy-start(bf16[27,256,256]{2,1,0:T(8,128)(2,1)} %fusion.1) | copy-start | bytes 10616836
  179.4 5.4 %collective-permute-start.7 = (f32[3,3,256,256]{3,2,1,0:T(8,128)S(1)}, f32[3,3,256,256]{3,2,1,0:T(8,128)S(1)}, u32[]{:S(2)}, u32[]{:S(2)}) collective-permute-start(f32[3,3,256,256]{3,2,1,0:T(8,128)S(1)} %bitcast.73), channel_id=1, source_target_pairs={{0,128},{1,129},{2,130},{3,131},{4,132},{5,133},{6,134},{7,135},{8... | collective-permute-start | bytes 7077896 | tf_op jit(solution)/shard_map/ppermute | solution.py:10
  180.8 6.4 %collective-permute-start.6 = (f32[3,3,256,256]{3,2,1,0:T(8,128)S(1)}, f32[3,3,256,256]{3,2,1,0:T(8,128)S(1)}, u32[]{:S(2)}, u32[]{:S(2)}) collective-permute-start(f32[3,3,256,256]{3,2,1,0:T(8,128)S(1)} %bitcast.70), channel_id=1, source_target_pairs={{128,0},{129,1},{130,2},{131,3},{132,4},{133,5},{134,6},{135,7},{1... | collective-permute-start | bytes 7077896 | tf_op jit(solution)/shard_map/ppermute | solution.py:10
  188.5 55.2 %collective-permute-start.9 = (f32[3,3,256,256]{3,2,1,0:T(8,128)S(1)}, f32[3,3,256,256]{3,2,1,0:T(8,128)S(1)}, u32[]{:S(2)}, u32[]{:S(2)}) collective-permute-start(f32[3,3,256,256]{3,2,1,0:T(8,128)S(1)} %get-tuple-element.10), channel_id=1, source_target_pairs={{0,32},{32,64},{64,96},{1,33},{33,65},{65,97},{2,34},{34,66},{66,9... | collective-permute-start | bytes 7077896 | tf_op jit(solution)/shard_map/ppermute | solution.py:10
  191.5 54.9 %collective-permute-start.8 = (f32[3,3,256,256]{3,2,1,0:T(8,128)S(1)}, f32[3,3,256,256]{3,2,1,0:T(8,128)S(1)}, u32[]{:S(2)}, u32[]{:S(2)}) collective-permute-start(f32[3,3,256,256]{3,2,1,0:T(8,128)S(1)} %get-tuple-element.9), channel_id=1, source_target_pairs={{32,0},{64,32},{96,64},{33,1},{65,33},{97,65},{34,2},{66,34},{98,6... | collective-permute-start | bytes 7077896 | tf_op jit(solution)/shard_map/ppermute | solution.py:10
  247.0 16.3 %copy-start.8 = (s32[1,1,1,256]{3,2,1,0:T(1,128)S(1)}, s32[1,1,1,256]{3,2,1,0:T(1,128)}, u32[]{:S(2)}) copy-start(s32[1,1,1,256]{3,2,1,0:T(1,128)} %param.16) | copy-start | bytes 3076
  248.9 124.4 %copy-start.4 = (f32[256,256]{1,0:T(8,128)}, f32[256,256]{1,0:T(8,128)S(1)}, u32[]{:S(2)}) copy-start(f32[256,256]{1,0:T(8,128)S(1)} %get-tuple-element.6) | copy-start | bytes 786436
  248.9 111.7 %collective-permute-start.11 = (f32[3,3,256,256]{3,2,0,1:T(8,128)S(1)}, f32[3,3,256,256]{3,2,0,1:T(8,128)}, u32[]{:S(2)}, u32[]{:S(2)}) collective-permute-start(f32[3,3,256,256]{3,2,0,1:T(8,128)S(1)} %get-tuple-element.7), channel_id=1, source_target_pairs={{0,1},{1,2},{2,3},{3,4},{4,5},{5,6},{6,7},{7,8},{8,9},{9,10},{10,1... | collective-permute-start | bytes 7077896 | tf_op jit(solution)/shard_map/ppermute | solution.py:10
  261.4 111.7 %collective-permute-start.10 = (f32[3,3,256,256]{3,2,0,1:T(8,128)}, f32[3,3,256,256]{3,2,0,1:T(8,128)S(1)}, u32[]{:S(2)}, u32[]{:S(2)}) collective-permute-start(f32[3,3,256,256]{3,2,0,1:T(8,128)} %get-tuple-element.8), channel_id=1, source_target_pairs={{1,0},{2,1},{3,2},{4,3},{5,4},{6,5},{7,6},{8,7},{9,8},{10,9},{11,1... | collective-permute-start | bytes 7077896 | tf_op jit(solution)/shard_map/ppermute | solution.py:10
  362.5 11.9 %copy-start.5 = (f32[256,256]{1,0:T(8,128)}, f32[256,256]{1,0:T(8,128)S(1)}, u32[]{:S(2)}) copy-start(f32[256,256]{1,0:T(8,128)S(1)} %reduce_sum.46) | copy-start | bytes 786436
  373.3 1.2 copy-start.6
  373.3 9.1 %copy-start.9 = (s32[1,1,16]{2,1,0:T(1,128)S(1)}, s32[1,1,16]{2,1,0:T(1,128)}, u32[]{:S(2)}) copy-start(s32[1,1,16]{2,1,0:T(1,128)} %param.17) | copy-start | bytes 196
  376.1 18.9 %copy-start.1 = (bf16[1,1,1,27,256,256]{5,4,3,2,1,0:T(8,128)(2,1)S(1)}, bf16[1,1,1,27,256,256]{5,4,3,2,1,0:T(8,128)(2,1)}, u32[]{:S(2)}) copy-start(bf16[1,1,1,27,256,256]{5,4,3,2,1,0:T(8,128)(2,1)} %param.10) | copy-start | bytes 10616836
  382.4 8.5 %collective-permute-start.12 = (f32[256,256]{0,1:T(8,128)}, f32[256,256]{0,1:T(8,128)}, u32[]{:S(2)}, u32[]{:S(2)}) collective-permute-start(f32[256,256]{0,1:T(8,128)} %bitcast_select_fusion), channel_id=1, source_target_pairs={{0,1},{1,0},{2,3},{3,2},{4,5},{5,4},{6,7},{7,6},{8,9},{9,8},{10,11... | collective-permute-start | bytes 786440 | tf_op jit(solution)/shard_map/ppermute | solution.py:37
where the time goes:
time: 396 us; the launch traced here: 395 us
  waiting for transfers between devices  289 us (73%)
  starting transfers between devices  47.5 us (12%)
  local copies, waits for them, and re-layouts  24.2 us (6%)
  matrix products  17.1 us (4%)
  other arithmetic  14.4 us (4%)
    ppermute x6, waiting for transfers between devices, shifted(): return lax.ppermute(block, axis, route)  165 us
    ppermute x3, waiting for transfers between devices, padded(): lax.ppermute(head, axis, [((i + 1) % count, i) for i in range(ends)])  115 us
    ppermute x6, starting transfers between devices, shifted(): return lax.ppermute(block, axis, route)  23.3 us
    ppermute x3, starting transfers between devices, padded(): lax.ppermute(tail, axis, [(i, (i + 1) % count) for i in range(ends)])  18.1 us
    dot_general x1, matrix products, on_device(): jnp.einsum('osr,ort->ost', upper, solved, preferred_element_type=jnp.floa...  13.1 us
  transfers between devices with their start and end apart: 13, of which 12 were waited for; matrix products, arithmetic and copies ran while one was open for 1% of the time, Pallas kernels for 0%

commit v1 on v0

v1 whole, which is shorter than its diff:
```python
import functools

import jax
import jax.numpy as jnp
from jax import lax
from jax.experimental import pallas as pl
from jax.experimental.pallas import tpu as pltpu
from jax.sharding import PartitionSpec as P

BF16 = jnp.bfloat16
F32 = jnp.float32
LIMIT = 16 * 1024 * 1024


def even_pairs(count):
    return [(i, i + 1) for i in range(0, count - 1, 2)]


def odd_pairs(count):
    return [(i, i + 1) for i in range(1, count - 1, 2)]


def swap(block, axis, pairs):
    route = []
    for low, high in pairs(lax.axis_size(axis)):
        route += [(low, high), (high, low)]
    return lax.ppermute(block, axis, route)


def dot(a, b):
    return jnp.dot(a, b, preferred_element_type=F32)


def dot_t(a, b):
    return lax.dot_general(a, b, (((1,), (1,)), ((), ())), preferred_element_type=F32)


def even_step(axis):
    return 1 - 2 * lax.rem(lax.axis_index(axis), 2)


def on_grid(axis, step):
    there = lax.axis_index(axis) + step
    return (there >= 0) & (there < lax.axis_size(axis))


def far_targets():
    y, z = even_step("by"), even_step("bz")
    return [(-z, y), (-z, -y), (-z, 0)]


def near_targets():
    y, z = even_step("by"), even_step("bz")
    return [(z, y), (z, -y), (z, 0), (0, y), (0, -y), (0, 0)]


def in_hbm(array):
    return pltpu.with_memory_space_constraint(array, pltpu.HBM)


def in_vmem(array):
    return pltpu.with_memory_space_constraint(array, pltpu.VMEM)


def call(kernel, inputs, outputs, scratch=(), flops=0, bytes_accessed=0, aliases=None):
    spaces = {"hbm": pltpu.HBM, "vmem": pltpu.VMEM, "smem": pltpu.SMEM}
    place = {"hbm": in_hbm, "vmem": in_vmem, "smem": lambda array: array}
    return pl.pallas_call(
        kernel,
        out_shape=tuple(outputs),
        in_specs=[pl.BlockSpec(memory_space=spaces[where]) for _, where in inputs],
        out_specs=tuple(
            pl.BlockSpec(memory_space=pltpu.HBM if isinstance(out, jax.ShapeDtypeStruct) else pltpu.VMEM)
            for out in outputs
        ),
        scratch_shapes=list(scratch),
        input_output_aliases=aliases or {},
        compiler_params=pltpu.CompilerParams(vmem_limit_bytes=LIMIT),
        cost_estimate=pl.CostEstimate(
            flops=flops, bytes_accessed=bytes_accessed, transcendentals=0
        ),
    )(*[place[where](array) for array, where in inputs])


def products(left, cols, start, order, store):
    size = cols.shape[1]
    for i, (z_step, y_step) in enumerate(order):
        inside = (on_grid("by", y_step) & on_grid("bz", z_step)).astype(F32)
        store(i, dot(left[i * size : (i + 1) * size], cols[start + i]) * inside)


def far_other_kernel(
    row_hbm, col_hbm, inverse_hbm, pivots_hbm, out, rows, cols, unpermuted, far_rows, far_cols, inverse, pivots, sems
):
    size = inverse.shape[0]
    other = even_step("bx")

    def place(x_step, step):
        z_step, y_step = step
        return 9 * (x_step + 1) + 3 * (y_step + 1) + (z_step + 1)

    def fetch(places, into_rows, into_cols, first):
        copies = []
        for i, at in enumerate(places):
            spot = into_rows.at[pl.ds(i * size, size), :]
            copies.append(
                (
                    pltpu.make_async_copy(row_hbm.at[at], spot, sems.at[0, first + i]),
                    pltpu.make_async_copy(col_hbm.at[at], into_cols.at[i], sems.at[1, first + i]),
                )
            )
        return copies

    head = [
        pltpu.make_async_copy(inverse_hbm, inverse, sems.at[0, 18]),
        pltpu.make_async_copy(pivots_hbm, pivots, sems.at[1, 18]),
    ]
    far = fetch([place(other, step) for step in far_targets()], far_rows, far_cols, 0)
    later = [place(other, step) for step in near_targets()]
    later += [place(0, step) for step in far_targets() + near_targets()]
    rest = fetch(later, rows, cols, 3)
    for copy in head:
        copy.start()
    for row_copy, _ in far:
        row_copy.start()
    for _, col_copy in far:
        col_copy.start()
    for row_copy, col_copy in rest:
        row_copy.start()
        col_copy.start()
    for copy in head:
        copy.wait()
    ids = lax.broadcasted_iota(jnp.int32, (size, size), 0)
    hot = (ids == pivots[...]).astype(F32).astype(BF16)
    unpermuted[...] = dot_t(inverse[...], hot).astype(BF16)
    for row_copy, _ in far:
        row_copy.wait()
    left = dot(far_rows[...], unpermuted[...]).astype(BF16)
    for _, col_copy in far:
        col_copy.wait()

    def store(i, value):
        out[i] = value.astype(BF16)

    products(left, far_cols, 0, far_targets(), store)
    for row_copy, col_copy in rest:
        row_copy.wait()
        col_copy.wait()


def near_other_kernel(rows, cols, unpermuted, out):
    left = dot(rows[0 : 6 * cols.shape[1], :], unpermuted[...]).astype(BF16)

    def store(i, value):
        out[i] = value.astype(BF16)

    products(left, cols, 0, near_targets(), store)


def own_kernel(rows, cols, unpermuted, far, near):
    left = dot(rows[6 * cols.shape[1] :, :], unpermuted[...]).astype(BF16)

    def store(i, value):
        if i < 3:
            far[i] = value
        else:
            near[i - 3] = value

    products(left, cols, 6, far_targets() + near_targets(), store)


def far_join_kernel(own, other, even, odd, keep):
    even[...] = (own[0] + other[0].astype(F32)).astype(BF16)
    odd[...] = (own[1] + other[1].astype(F32)).astype(BF16)
    keep[...] = own[2] + other[2].astype(F32)


def near_join_kernel(own, other, after, out, keep):
    del after
    out[...] = (own[0:3] + other[0:3].astype(F32)).astype(BF16)
    keep[...] = own[3:6] + other[3:6].astype(F32)


def far_kernel(keep, even, odd, out):
    out[...] = (keep[...] + even[...].astype(F32) + odd[...].astype(F32)).astype(BF16)


def near_kernel(center, side, even, odd, keep):
    total = center[...] + side[...].astype(F32)
    even[...] = total[0].astype(BF16)
    odd[...] = total[1].astype(BF16)
    keep[...] = total[2]


def select_kernel(
    count_ref, skel_hbm, order_hbm, self_hbm, rows_out, cols_out, chosen_out, self_vmem, skel, order, sems
):
    copies = [
        pltpu.make_async_copy(skel_hbm, skel, sems.at[0]),
        pltpu.make_async_copy(order_hbm, order, sems.at[1]),
        pltpu.make_async_copy(self_hbm, self_vmem, sems.at[2]),
    ]
    for copy in copies:
        copy.start()
    size = self_vmem.shape[0]
    count = count_ref[0]
    points = lax.broadcasted_iota(jnp.int32, (size, size), 0)
    lanes = lax.broadcasted_iota(jnp.int32, (size, size), 1)
    live = (points < count).astype(F32)
    for copy in copies:
        copy.wait()
    rows = (skel[0].astype(F32) * live).astype(BF16)
    cols = (skel[1].astype(F32) * live).astype(BF16)
    hot_t = ((points == order[...]) & (lanes < count)).astype(F32)
    hot = hot_t.T.astype(BF16)
    hot_t = hot_t.astype(BF16)

    def parts(value):
        high = value.astype(BF16)
        rest = value - high.astype(F32)
        middle = rest.astype(BF16)
        return high, middle, (rest - middle.astype(F32)).astype(BF16)

    high, middle, low = parts(self_vmem[...])
    picked = dot(hot, jnp.concatenate([rows, cols, high, middle, low], axis=1))
    rows_out[0:size, :] = rows
    rows_out[size:, :] = picked[:, :size].astype(BF16)
    cols_out[0] = cols
    cols_out[1] = picked[:, size : 2 * size].astype(BF16)
    by_row = (
        picked[:, 2 * size : 3 * size] + picked[:, 3 * size : 4 * size] + picked[:, 4 * size :]
    )
    both = dot(jnp.concatenate(parts(by_row), axis=0), hot_t)
    chosen_out[...] = both[:size] + both[size : 2 * size] + both[2 * size :]


def child_kernel(kept, even, odd, far, rows, cols, chosen, total_out, child, child_sent):
    size = chosen.shape[0]
    total = kept[...] + even[...].astype(F32) + odd[...].astype(F32) + far[...].astype(F32)
    total = total.astype(BF16)
    total_out[...] = total
    left = dot(rows[size:, :], total).astype(BF16)
    picked = chosen[...] - dot_t(left, cols[1])
    child[...] = picked
    child_sent[...] = picked.astype(BF16)


def owner_of_pair(owner):
    zpos = lax.axis_index("bz")
    parity = lax.rem(zpos, 2)
    return parity, (owner[0, 0, lax.div(zpos, 2)] == parity).astype(F32)


def update_kernel(owner, total, rows, cols, own_self, child, updated_hbm, parent_hbm, updated, mine, sems):
    size = own_self.shape[0]
    parity, owns = owner_of_pair(owner)
    mine[...] = child[...] * owns
    first = pltpu.make_async_copy(mine, parent_hbm.at[parity], sems.at[0])
    first.start()
    left = dot(rows[0:size, :], total[...]).astype(BF16)
    updated[...] = own_self[...] - dot_t(left, cols[0])
    second = pltpu.make_async_copy(updated, updated_hbm, sems.at[1])
    second.start()
    first.wait()
    second.wait()


def parent_kernel(owner, partner, parent_in, parent_hbm, theirs, sem):
    del parent_in
    parity, owns = owner_of_pair(owner)
    theirs[...] = partner[...].astype(F32) * owns
    copy = pltpu.make_async_copy(theirs, parent_hbm.at[1 - parity], sem)
    copy.start()
    copy.wait()


def on_device(
    skel_blocks,
    row_couple,
    col_couple,
    inverse_rr,
    pivots,
    self_block,
    skel_count,
    skel_order,
    owner_flag,
):
    size = inverse_rr.shape[-1]
    block = (size, size)
    row_couple = row_couple.reshape(row_couple.shape[-3:])
    col_couple = col_couple.reshape(col_couple.shape[-3:])
    inverse = inverse_rr.reshape(block)
    pivots = pivots.reshape(1, size)

    far_other, later_rows, later_cols, unpermuted = call(
        far_other_kernel,
        [(row_couple, "hbm"), (col_couple, "hbm"), (inverse, "hbm"), (pivots, "hbm")],
        [
            pltpu.VMEM((3, *block), BF16),
            pltpu.VMEM((15 * size, size), BF16),
            pltpu.VMEM((15, *block), BF16),
            pltpu.VMEM(block, BF16),
        ],
        [
            pltpu.VMEM((3 * size, size), BF16),
            pltpu.VMEM((3, *block), BF16),
            pltpu.VMEM(block, BF16),
            pltpu.VMEM((1, size), jnp.int32),
            pltpu.SemaphoreType.DMA((2, 19)),
        ],
        flops=14 * size**3,
        bytes_accessed=36 * 2 * size * size,
    )
    far_other = swap(far_other, "bx", even_pairs)
    later = [(later_rows, "vmem"), (later_cols, "vmem"), (unpermuted, "vmem")]
    (near_other,) = call(
        near_other_kernel,
        later,
        [pltpu.VMEM((6, *block), BF16)],
        flops=24 * size**3,
        bytes_accessed=36 * size * size,
    )
    near_other = swap(near_other, "bx", even_pairs)
    far_own, near_own = call(
        own_kernel,
        later,
        [pltpu.VMEM((3, *block), F32), pltpu.VMEM((6, *block), F32)],
        flops=36 * size**3,
        bytes_accessed=72 * size * size,
    )
    far_even, far_odd, far_keep = call(
        far_join_kernel,
        [(far_own, "vmem"), (far_other, "vmem")],
        [pltpu.VMEM(block, BF16), pltpu.VMEM(block, BF16), pltpu.VMEM(block, F32)],
        flops=3 * size * size,
        bytes_accessed=26 * size * size,
    )
    far_even = swap(far_even, "by", even_pairs)
    far_odd = swap(far_odd, "by", odd_pairs)
    side, center = call(
        near_join_kernel,
        [(near_own, "vmem"), (near_other, "vmem"), (far_keep, "vmem")],
        [pltpu.VMEM((3, *block), BF16), pltpu.VMEM((3, *block), F32)],
        flops=6 * size * size,
        bytes_accessed=54 * size * size,
    )
    side = swap(side, "bz", even_pairs)

    rows, cols, chosen, own_self = call(
        select_kernel,
        [
            (skel_count.reshape(1), "smem"),
            (skel_blocks.reshape(2, size, size), "hbm"),
            (skel_order.reshape(1, size), "hbm"),
            (self_block.reshape(block), "hbm"),
        ],
        [
            pltpu.VMEM((2 * size, size), BF16),
            pltpu.VMEM((2, size, size), BF16),
            pltpu.VMEM(block, F32),
            pltpu.VMEM(block, F32),
        ],
        [
            pltpu.VMEM((2, size, size), BF16),
            pltpu.VMEM((1, size), jnp.int32),
            pltpu.SemaphoreType.DMA((3,)),
        ],
        flops=16 * size**3,
        bytes_accessed=20 * size * size,
    )

    (far,) = call(
        far_kernel,
        [(far_keep, "vmem"), (far_even, "vmem"), (far_odd, "vmem")],
        [pltpu.VMEM(block, BF16)],
        flops=2 * size * size,
        bytes_accessed=10 * size * size,
    )
    far = swap(far, "bz", odd_pairs)
    near_even, near_odd, kept = call(
        near_kernel,
        [(center, "vmem"), (side, "vmem")],
        [pltpu.VMEM(block, BF16), pltpu.VMEM(block, BF16), pltpu.VMEM(block, F32)],
        flops=3 * size * size,
        bytes_accessed=26 * size * size,
    )
    near_even = swap(near_even, "by", even_pairs)
    near_odd = swap(near_odd, "by", odd_pairs)

    total, child, child_sent = call(
        child_kernel,
        [
            (kept, "vmem"),
            (near_even, "vmem"),
            (near_odd, "vmem"),
            (far, "vmem"),
            (rows, "vmem"),
            (cols, "vmem"),
            (chosen, "vmem"),
        ],
        [pltpu.VMEM(block, BF16), pltpu.VMEM(block, F32), pltpu.VMEM(block, BF16)],
        flops=4 * size**3,
        bytes_accessed=28 * size * size,
    )
    partner = swap(child_sent, "bz", even_pairs)
    updated, parent = call(
        update_kernel,
        [
            (owner_flag, "smem"),
            (total, "vmem"),
            (rows, "vmem"),
            (cols, "vmem"),
            (own_self, "vmem"),
            (child, "vmem"),
        ],
        [jax.ShapeDtypeStruct(block, F32), jax.ShapeDtypeStruct((2, *block), F32)],
        [pltpu.VMEM(block, F32), pltpu.VMEM(block, F32), pltpu.SemaphoreType.DMA((2,))],
        flops=4 * size**3,
        bytes_accessed=28 * size * size,
    )
    (parent,) = call(
        parent_kernel,
        [(owner_flag, "smem"), (partner, "vmem"), (parent, "hbm")],
        [jax.ShapeDtypeStruct((2, *block), F32)],
        [pltpu.VMEM(block, F32), pltpu.SemaphoreType.DMA],
        flops=size * size,
        bytes_accessed=6 * size * size,
        aliases={2: 0},
    )
    return (updated[None, None, None], parent[None, None, None])


def solution(mesh):
    in_specs = (
        P("bx", "by", "bz", None, None, None),
        P("bx", "by", "bz", None, None, None),
        P("bx", "by", "bz", None, None, None),
        P("bx", "by", "bz", None, None),
        P("bx", "by", "bz", None),
        P("bx", "by", "bz", None, None),
        P("bx", "by", "bz"),
        P("bx", "by", "bz", None),
        P("bx", "by", None),
    )
    out_specs = (P("bx", "by", "bz", None, None), P("bx", "by", "bz", None, None, None))
    return jax.shard_map(
        on_device, mesh=mesh, in_specs=in_specs, out_specs=out_specs, check_vma=False
    )
```

time: 396 us -> 41.1 us (0.10)
  waiting for transfers between devices: 289 us -> 12 us
  starting transfers between devices: 47.5 us -> 17.7 us
  local copies, waits for them, and re-layouts: 24.2 us -> 0.01 us
  matrix products: 17.1 us -> 0 us
  other arithmetic: 14.4 us -> 0 us
  Pallas kernels: 0 us -> 9.72 us
    ppermute x13 -> x9, waiting for transfers between devices: 289 us -> 12 us  [swap(): return lax.ppermute(block, axis, route)]
    ppermute x13 -> x9, starting transfers between devices: 47.5 us -> 17.7 us  [swap(): return lax.ppermute(block, axis, route)]
    dot_general x3 -> x0, matrix products: 17.1 us -> none  [the longest x1 13.1 us: on_device(): jnp.einsum('osr,ort->ost', upper, solved, preferred_element_type=jnp.floa...]
    gather x4 -> x0, local copies, waits for them, and re-layouts: 11.3 us -> none  [the longest x3 6.19 us: on_device(): chosen = updated[order][:, order]]
    pallas_call x0 -> x11, Pallas kernels: none -> 9.72 us  [call(): pl.pallas_call(kernel, out_shape=tuple(outputs), in_specs=[pl.BlockSpec(m...]
    dot_general x1 -> x0, local copies, waits for them, and re-layouts: 6.07 us -> none  [on_device(): jnp.einsum('orq,osq->ors', col_couple[0, 0, 0], nearby[:, 1], preferred_e...]
  transfers between devices with their start and end apart: 13 -> 9, of which waited for: 12 -> 4; matrix products, arithmetic and copies ran while one was open for 1% -> 0% of each run, Pallas kernels for 0% -> 11%
where the time goes in v1:
time: 41.1 us; the launch traced here: 40.9 us
  starting transfers between devices  17.7 us (43%)
  waiting for transfers between devices  12 us (29%)
  Pallas kernels  9.72 us (24%)
  between operations  1.43 us (3%)
    ppermute x9, starting transfers between devices, swap(): return lax.ppermute(block, axis, route)  17.7 us
    ppermute x9, waiting for transfers between devices, swap(): return lax.ppermute(block, axis, route)  12 us
    pallas_call x11, Pallas kernels, call(): pl.pallas_call(kernel, out_shape=tuple(outputs), in_specs=[pl.BlockSpec(m...  9.72 us
  transfers between devices with their start and end apart: 9, of which 4 were waited for; matrix products, arithmetic and copies ran while one was open for 0% of the time, Pallas kernels for 11%

profile of v1, /device:TPU:62, one launch (start us, length us, event | category | flops | bytes accessed | tf_op | source)
XLA Modules:
  0.0 40.9 jit_solution(7825753665035805836)
XLA Ops:
  0.6 2.8 %shard_map.104 = (bf16[3,256,256]{2,1,0:T(8,128)(2,1)S(1)}, bf16[3840,256]{1,0:T(8,128)(2,1)S(1)}, bf16[15,256,256]{2,1,0:T(8,128)(2,1)S(1)}, bf16[256,256]{1,0:T(8,128)(2,1)S(1)}) custom-call(bf16[27,256,256]{2,1,0:T(8,128)(2,1)} %bitcast.11, bf16[27,256,256]{2,1,0:T(8,128)(2,1)} %bitcast.12, bf16[256,256]{1,0:T(8,128)(2,1)} %bitcast.14, s32[1,256]{1,0:T(1,128)} %bitcast.15), custom_call_target="tpu_custom_call" | custom-call | flops 234881024 | bytes 4718592 | tf_op jit(solution)/shard_map/pallas_call | solution.py:68
  3.4 0.7 %shard_map.106 = bf16[6,256,256]{2,1,0:T(8,128)(2,1)S(1)} custom-call(bf16[3840,256]{1,0:T(8,128)(2,1)S(1)} %get-tuple-element.25.rows, bf16[15,256,256]{2,1,0:T(8,128)(2,1)S(1)} %get-tuple-element.26.cols, bf16[256,256]{1,0:T(8,128)(2,1)S(1)} %get-tuple-element.27.unpermuted), custom_call_target="tpu_custom_call" | custom-call | flops 402653184 | bytes 2359296 | tf_op jit(solution)/shard_map/pallas_call | solution.py:68
  4.1 0.1 collective-permute-start
  4.2 0.5 %collective-permute-start.1 = (bf16[3,256,256]{2,1,0:T(8,128)(2,1)S(1)}, bf16[3,256,256]{2,1,0:T(8,128)(2,1)S(1)}, u32[]{:S(2)}, u32[]{:S(2)}) collective-permute-start(bf16[3,256,256]{2,1,0:T(8,128)(2,1)S(1)} %get-tuple-element.30), channel_id=1, source_target_pairs={{0,128},{128,0},{1,129},{129,1},{2,130},{130,2},{3,131},{131,3},{4... | collective-permute-start | bytes 1179656 | tf_op jit(solution)/shard_map/ppermute | solution.py:27
  4.7 0.9 %shard_map.105 = (f32[3,256,256]{2,1,0:T(8,128)S(1)}, f32[6,256,256]{2,1,0:T(8,128)S(1)}) custom-call(bf16[3840,256]{1,0:T(8,128)(2,1)S(1)} %get-tuple-element.25.rows, bf16[15,256,256]{2,1,0:T(8,128)(2,1)S(1)} %get-tuple-element.26.cols, bf16[256,256]{1,0:T(8,128)(2,1)S(1)} %get-tuple-element.27.unpermuted), custom_call_target="tpu_custom_call" | custom-call | flops 603979776 | bytes 4718592 | tf_op jit(solution)/shard_map/pallas_call | solution.py:68
  5.6 1.5 %collective-permute-done.1.other = bf16[3,256,256]{2,1,0:T(8,128)(2,1)S(1)} collective-permute-done((bf16[3,256,256]{2,1,0:T(8,128)(2,1)S(1)}, bf16[3,256,256]{2,1,0:T(8,128)(2,1)S(1)}, u32[]{:S(2)}, u32[]{:S(2)}) %collective-permute-start.1) | collective-permute-done | bytes 393248 | tf_op jit(solution)/shard_map/ppermute | solution.py:27
  7.0 0.1 shard_map.107
  7.1 0.1 shard_map.108
  7.2 0.9 %collective-permute-start.2 = (bf16[3,256,256]{2,1,0:T(8,128)(2,1)S(1)}, bf16[3,256,256]{2,1,0:T(8,128)(2,1)S(1)}, u32[]{:S(2)}, u32[]{:S(2)}) collective-permute-start(bf16[3,256,256]{2,1,0:T(8,128)(2,1)S(1)} %get-tuple-element.33), channel_id=1, source_target_pairs={{0,1},{1,0},{2,3},{3,2},{4,5},{5,4},{6,7},{7,6},{8,9},{9,8},{10,11... | collective-permute-start | bytes 1179656 | tf_op jit(solution)/shard_map/ppermute | solution.py:27
  8.2 0.1 collective-permute-start.5
  8.3 5.6 %collective-permute-start.6 = (bf16[256,256]{1,0:T(8,128)(2,1)S(1)}, bf16[256,256]{1,0:T(8,128)(2,1)S(1)}, u32[]{:S(2)}, u32[]{:S(2)}) collective-permute-start(bf16[256,256]{1,0:T(8,128)(2,1)S(1)} %get-tuple-element.38), channel_id=1, source_target_pairs={{32,64},{64,32},{33,65},{65,33},{34,66},{66,34},{35,67},{67,35},{3... | collective-permute-start | bytes 393224 | tf_op jit(solution)/shard_map/ppermute | solution.py:27
  13.9 3.2 %collective-permute-done.6.odd = bf16[256,256]{1,0:T(8,128)(2,1)S(1)} collective-permute-done((bf16[256,256]{1,0:T(8,128)(2,1)S(1)}, bf16[256,256]{1,0:T(8,128)(2,1)S(1)}, u32[]{:S(2)}, u32[]{:S(2)}) %collective-permute-start.6) | collective-permute-done | bytes 131104 | tf_op jit(solution)/shard_map/ppermute | solution.py:27
  17.2 0.0 copy-start
  17.2 7.3 %collective-permute-start.7 = (bf16[256,256]{1,0:T(8,128)(2,1)S(1)}, bf16[256,256]{1,0:T(8,128)(2,1)S(1)}, u32[]{:S(2)}, u32[]{:S(2)}) collective-permute-start(bf16[256,256]{1,0:T(8,128)(2,1)S(1)} %shard_map.110), channel_id=1, source_target_pairs={{1,2},{2,1},{3,4},{4,3},{5,6},{6,5},{7,8},{8,7},{9,10},{10,9},{11,... | collective-permute-start | bytes 393224 | tf_op jit(solution)/shard_map/ppermute | solution.py:27
  24.5 0.1 shard_map.109
  24.6 0.1 collective-permute-start.3
  24.7 2.9 %collective-permute-start.4 = (bf16[256,256]{1,0:T(8,128)(2,1)S(1)}, bf16[256,256]{1,0:T(8,128)(2,1)S(1)}, u32[]{:S(2)}, u32[]{:S(2)}) collective-permute-start(bf16[256,256]{1,0:T(8,128)(2,1)S(1)} %get-tuple-element.36), channel_id=1, source_target_pairs={{32,64},{64,32},{33,65},{65,33},{34,66},{66,34},{35,67},{67,35},{3... | collective-permute-start | bytes 393224 | tf_op jit(solution)/shard_map/ppermute | solution.py:27
  28.3 1.8 %shard_map.111 = (bf16[512,256]{1,0:T(8,128)(2,1)S(1)}, bf16[2,256,256]{2,1,0:T(8,128)(2,1)S(1)}, f32[256,256]{1,0:T(8,128)S(1)}, f32[256,256]{1,0:T(8,128)S(1)}) custom-call(s32[1]{0:T(128)} %bitcast.10.count_ref, bf16[2,256,256]{2,1,0:T(8,128)(2,1)} %bitcast.16, s32[1,256]{1,0:T(1,128)} %bitcast.19, f32[256,256]{1,0:T(8,128)} %bitcast.17), custom_call_target="tpu_custom_call" | custom-call | flops 268435456 | bytes 1310720 | tf_op jit(solution)/shard_map/pallas_call | solution.py:68
  30.1 4.0 %collective-permute-done.7.far = bf16[256,256]{1,0:T(8,128)(2,1)S(1)} collective-permute-done((bf16[256,256]{1,0:T(8,128)(2,1)S(1)}, bf16[256,256]{1,0:T(8,128)(2,1)S(1)}, u32[]{:S(2)}, u32[]{:S(2)}) %collective-permute-start.7) | collective-permute-done | bytes 131104 | tf_op jit(solution)/shard_map/ppermute | solution.py:27
  34.2 0.4 shard_map.112
  34.5 0.1 collective-permute-start.8
  34.6 1.6 %shard_map.113 = (f32[256,256]{1,0:T(8,128)}, f32[2,256,256]{2,1,0:T(8,128)}) custom-call(s32[1,1,16]{2,1,0:T(1,128)S(1)} %copy-done, bf16[256,256]{1,0:T(8,128)(2,1)S(1)} %get-tuple-element.42.total, bf16[512,256]{1,0:T(8,128)(2,1)S(1)} %get-tuple-element.39.rows, bf16[2,256,256]{2,1,0:T(8,128)(2,1)S(1)} %get-tuple-element.40.cols, ...), custom_call_target="tpu_custom_call" | custom-call | flops 67108864 | bytes 1835008 | tf_op jit(solution)/shard_map/pallas_call | solution.py:68
  36.3 3.3 %collective-permute-done.8.partner = bf16[256,256]{1,0:T(8,128)(2,1)S(1)} collective-permute-done((bf16[256,256]{1,0:T(8,128)(2,1)S(1)}, bf16[256,256]{1,0:T(8,128)(2,1)S(1)}, u32[]{:S(2)}, u32[]{:S(2)}) %collective-permute-start.8) | collective-permute-done | bytes 131104 | tf_op jit(solution)/shard_map/ppermute | solution.py:27
  39.6 1.3 %shard_map.114 = f32[2,256,256]{2,1,0:T(8,128)} custom-call(s32[1,1,16]{2,1,0:T(1,128)S(1)} %copy-done, bf16[256,256]{1,0:T(8,128)(2,1)S(1)} %collective-permute-done.8.partner, f32[2,256,256]{2,1,0:T(8,128)} %get-tuple-element.47.parent_in), custom_call_target="tpu_custom_call", output_to_operand_aliasing={{}: (2, {})} | custom-call | flops 65536 | bytes 393216 | tf_op jit(solution)/shard_map/pallas_call | solution.py:68
  (7 shorter events, 0.1 us)
Async XLA Ops:
  4.1 3.0 %collective-permute-start = (bf16[6,256,256]{2,1,0:T(8,128)(2,1)S(1)}, bf16[6,256,256]{2,1,0:T(8,128)(2,1)S(1)}, u32[]{:S(2)}, u32[]{:S(2)}) collective-permute-start(bf16[6,256,256]{2,1,0:T(8,128)(2,1)S(1)} %shard_map.106), channel_id=1, source_target_pairs={{0,128},{128,0},{1,129},{129,1},{2,130},{130,2},{3,131},{131,3},{4... | collective-permute-start | bytes 2359304 | tf_op jit(solution)/shard_map/ppermute | solution.py:27
  4.2 2.8 %collective-permute-start.1 = (bf16[3,256,256]{2,1,0:T(8,128)(2,1)S(1)}, bf16[3,256,256]{2,1,0:T(8,128)(2,1)S(1)}, u32[]{:S(2)}, u32[]{:S(2)}) collective-permute-start(bf16[3,256,256]{2,1,0:T(8,128)(2,1)S(1)} %get-tuple-element.30), channel_id=1, source_target_pairs={{0,128},{128,0},{1,129},{129,1},{2,130},{130,2},{3,131},{131,3},{4... | collective-permute-start | bytes 1179656 | tf_op jit(solution)/shard_map/ppermute | solution.py:27
  7.2 17.3 %collective-permute-start.2 = (bf16[3,256,256]{2,1,0:T(8,128)(2,1)S(1)}, bf16[3,256,256]{2,1,0:T(8,128)(2,1)S(1)}, u32[]{:S(2)}, u32[]{:S(2)}) collective-permute-start(bf16[3,256,256]{2,1,0:T(8,128)(2,1)S(1)} %get-tuple-element.33), channel_id=1, source_target_pairs={{0,1},{1,0},{2,3},{3,2},{4,5},{5,4},{6,7},{7,6},{8,9},{9,8},{10,11... | collective-permute-start | bytes 1179656 | tf_op jit(solution)/shard_map/ppermute | solution.py:27
  8.2 5.7 %collective-permute-start.5 = (bf16[256,256]{1,0:T(8,128)(2,1)S(1)}, bf16[256,256]{1,0:T(8,128)(2,1)S(1)}, u32[]{:S(2)}, u32[]{:S(2)}) collective-permute-start(bf16[256,256]{1,0:T(8,128)(2,1)S(1)} %get-tuple-element.37), channel_id=1, source_target_pairs={{0,32},{32,0},{64,96},{96,64},{1,33},{33,1},{65,97},{97,65},{2,34}... | collective-permute-start | bytes 393224 | tf_op jit(solution)/shard_map/ppermute | solution.py:27
  8.3 8.9 %collective-permute-start.6 = (bf16[256,256]{1,0:T(8,128)(2,1)S(1)}, bf16[256,256]{1,0:T(8,128)(2,1)S(1)}, u32[]{:S(2)}, u32[]{:S(2)}) collective-permute-start(bf16[256,256]{1,0:T(8,128)(2,1)S(1)} %get-tuple-element.38), channel_id=1, source_target_pairs={{32,64},{64,32},{33,65},{65,33},{34,66},{66,34},{35,67},{67,35},{3... | collective-permute-start | bytes 393224 | tf_op jit(solution)/shard_map/ppermute | solution.py:27
  17.2 17.5 %copy-start = (s32[1,1,16]{2,1,0:T(1,128)S(1)}, s32[1,1,16]{2,1,0:T(1,128)}, u32[]{:S(2)}) copy-start(s32[1,1,16]{2,1,0:T(1,128)} %owner.3) | copy-start | bytes 196
  17.2 17.0 %collective-permute-start.7 = (bf16[256,256]{1,0:T(8,128)(2,1)S(1)}, bf16[256,256]{1,0:T(8,128)(2,1)S(1)}, u32[]{:S(2)}, u32[]{:S(2)}) collective-permute-start(bf16[256,256]{1,0:T(8,128)(2,1)S(1)} %shard_map.110), channel_id=1, source_target_pairs={{1,2},{2,1},{3,4},{4,3},{5,6},{6,5},{7,8},{8,7},{9,10},{10,9},{11,... | collective-permute-start | bytes 393224 | tf_op jit(solution)/shard_map/ppermute | solution.py:27
  24.6 9.5 %collective-permute-start.3 = (bf16[256,256]{1,0:T(8,128)(2,1)S(1)}, bf16[256,256]{1,0:T(8,128)(2,1)S(1)}, u32[]{:S(2)}, u32[]{:S(2)}) collective-permute-start(bf16[256,256]{1,0:T(8,128)(2,1)S(1)} %get-tuple-element.35), channel_id=1, source_target_pairs={{0,32},{32,0},{64,96},{96,64},{1,33},{33,1},{65,97},{97,65},{2,34}... | collective-permute-start | bytes 393224 | tf_op jit(solution)/shard_map/ppermute | solution.py:27
  24.7 9.4 %collective-permute-start.4 = (bf16[256,256]{1,0:T(8,128)(2,1)S(1)}, bf16[256,256]{1,0:T(8,128)(2,1)S(1)}, u32[]{:S(2)}, u32[]{:S(2)}) collective-permute-start(bf16[256,256]{1,0:T(8,128)(2,1)S(1)} %get-tuple-element.36), channel_id=1, source_target_pairs={{32,64},{64,32},{33,65},{65,33},{34,66},{66,34},{35,67},{67,35},{3... | collective-permute-start | bytes 393224 | tf_op jit(solution)/shard_map/ppermute | solution.py:27
  34.5 5.1 %collective-permute-start.8 = (bf16[256,256]{1,0:T(8,128)(2,1)S(1)}, bf16[256,256]{1,0:T(8,128)(2,1)S(1)}, u32[]{:S(2)}, u32[]{:S(2)}) collective-permute-start(bf16[256,256]{1,0:T(8,128)(2,1)S(1)} %get-tuple-element.46), channel_id=1, source_target_pairs={{0,1},{1,0},{2,3},{3,2},{4,5},{5,4},{6,7},{7,6},{8,9},{9,8},{10,11... | collective-permute-start | bytes 393224 | tf_op jit(solution)/shard_map/ppermute | solution.py:27

commit v2 on v1

v2 whole, which is shorter than its diff:
```python
import functools

import jax
import jax.numpy as jnp
from jax import lax
from jax.experimental import pallas as pl
from jax.experimental.pallas import tpu as pltpu
from jax.sharding import PartitionSpec as P

BF16 = jnp.bfloat16
F32 = jnp.float32
LIMIT = 16 * 1024 * 1024
HINT = 20 * 10**9


def swap_x(block):
    return lax.ppermute(block, "bx", [(0, 1), (1, 0)])


def swap_even(block, axis):
    route = []
    for low in range(0, lax.axis_size(axis) - 1, 2):
        route += [(low, low + 1), (low + 1, low)]
    return lax.ppermute(block, axis, route)


def swap_odd(block, axis):
    count = lax.axis_size(axis)
    route = []
    for x in (0, 1):
        for low in range(1, count - 1, 2):
            here, there = x * count + low, x * count + low + 1
            route += [(here, there), (there, here)]
        for end in (0, count - 1):
            route.append((x * count + end, (1 - x) * count + end))
    return lax.ppermute(block, ("bx", axis), route)


def swap_y(blocks):
    count = lax.axis_size("by")
    out = []
    for low, block in enumerate(blocks):
        route = []
        for x in (0, 1):
            for y in range(count):
                if y == low:
                    there = (x, y + 1)
                elif y == low + 1:
                    there = (x, y - 1)
                else:
                    there = (1 - x, y)
                route.append((x * count + y, there[0] * count + there[1]))
        out.append(lax.ppermute(block, ("bx", "by"), route))
    return out


def toward(pair):
    return jnp.where(lax.axis_index("by") == pair, 2, 0)


def received(pair, block):
    y = lax.axis_index("by")
    return block.astype(F32) * ((y == pair) | (y == pair + 1)).astype(F32)


def dot(a, b):
    return jnp.dot(a, b, preferred_element_type=F32)


def dot_t(a, b):
    return lax.dot_general(a, b, (((1,), (1,)), ((), ())), preferred_element_type=F32)


def even_step(axis):
    return 1 - 2 * lax.rem(lax.axis_index(axis), 2)


def on_grid(axis, step):
    there = lax.axis_index(axis) + step
    return (there >= 0) & (there < lax.axis_size(axis))


def in_hbm(array):
    return pltpu.with_memory_space_constraint(array, pltpu.HBM)


def in_vmem(array):
    return pltpu.with_memory_space_constraint(array, pltpu.VMEM)


def call(kernel, inputs, outputs, scratch=(), aliases=None, hint=0):
    spaces = {"hbm": pltpu.HBM, "vmem": pltpu.VMEM, "smem": pltpu.SMEM}
    place = {"hbm": in_hbm, "vmem": in_vmem, "smem": lambda array: array}
    return pl.pallas_call(
        kernel,
        out_shape=tuple(outputs),
        in_specs=[pl.BlockSpec(memory_space=spaces[where]) for _, where in inputs],
        out_specs=tuple(
            pl.BlockSpec(memory_space=pltpu.HBM if isinstance(out, jax.ShapeDtypeStruct) else pltpu.VMEM)
            for out in outputs
        ),
        scratch_shapes=list(scratch),
        input_output_aliases=aliases or {},
        compiler_params=pltpu.CompilerParams(vmem_limit_bytes=LIMIT),
        cost_estimate=pl.CostEstimate(
            flops=hint, bytes_accessed=0, transcendentals=0
        ),
    )(*[place[where](array) for array, where in inputs])


def z_steps():
    z = even_step("bz")
    return -z, z, 0


def products(rows, cols, unpermuted, steps, store):
    size = unpermuted.shape[0]
    count = 3 * len(steps)
    left = dot(rows.reshape(count * size, size), unpermuted).astype(BF16)
    for i in range(count):
        inside = on_grid("bz", steps[i // 3]).astype(F32)
        store(i, dot(left[i * size : (i + 1) * size], cols[i]) * inside)


def fetch(row_hbm, col_hbm, x, z, rows, cols, sems, at):
    return (
        pltpu.make_async_copy(row_hbm.at[x + 1, :, z + 1], rows, sems.at[0, at]),
        pltpu.make_async_copy(col_hbm.at[x + 1, :, z + 1], cols, sems.at[1, at]),
    )


def first_kernel(
    row_hbm, col_hbm, inverse_hbm, pivots_hbm, other, own, rows, cols, own_rows, own_cols, unpermuted, far_rows, far_cols, inverse, pivots, sems
):
    size = inverse.shape[0]
    x_step = even_step("bx")
    far, near, center = z_steps()
    low, high = pl.ds(0, 3), pl.ds(3, 3)
    head = (
        pltpu.make_async_copy(inverse_hbm, inverse, sems.at[0, 6]),
        pltpu.make_async_copy(pivots_hbm, pivots, sems.at[1, 6]),
    )
    far_other = fetch(row_hbm, col_hbm, x_step, far, far_rows.at[low], far_cols.at[low], sems, 0)
    far_own = fetch(row_hbm, col_hbm, 0, far, far_rows.at[high], far_cols.at[high], sems, 1)
    rest = fetch(row_hbm, col_hbm, x_step, near, rows.at[low], cols.at[low], sems, 2)
    rest += fetch(row_hbm, col_hbm, x_step, center, rows.at[high], cols.at[high], sems, 3)
    rest += fetch(row_hbm, col_hbm, 0, near, own_rows, own_cols, sems, 4)
    for copy in head + far_other + far_own + rest:
        copy.start()
    for copy in head:
        copy.wait()
    ids = lax.broadcasted_iota(jnp.int32, (size, size), 0)
    hot = (ids == pivots[...]).astype(F32).astype(BF16)
    unpermuted[...] = dot_t(inverse[...], hot).astype(BF16)

    def store_other(i, value):
        other[i] = value.astype(BF16)

    def store_own(i, value):
        own[i] = value

    for copy in far_other:
        copy.wait()
    products(far_rows[0:3], far_cols.at[low], unpermuted[...], [far], store_other)
    for copy in far_own:
        copy.wait()
    products(far_rows[3:6], far_cols.at[high], unpermuted[...], [far], store_own)
    for copy in rest:
        copy.wait()


def near_other_kernel(row_hbm, col_hbm, rows, cols, unpermuted, out, center_rows, center_cols, sems):
    copies = fetch(row_hbm, col_hbm, 0, 0, center_rows, center_cols, sems, 0)
    for copy in copies:
        copy.start()

    def store(i, value):
        out[i] = value.astype(BF16)

    products(rows[...], cols, unpermuted[...], z_steps()[1:], store)
    for copy in copies:
        copy.wait()


def far_join_kernel(own, other, first, second, third, keep):
    for pair, out in enumerate((first, second, third)):
        at = toward(pair)
        out[...] = (own[at] + other[at].astype(F32)).astype(BF16)
    keep[...] = own[1] + other[1].astype(F32)


def near_join_kernel(rows, cols, center_rows, center_cols, unpermuted, other, after, outer, middle, center):
    del after

    def store(i, value):
        total = value + other[i].astype(F32)
        if i == 1:
            middle[...] = total.astype(BF16)
        elif i < 3:
            outer[i // 2] = total.astype(BF16)
        else:
            center[i - 3] = total

    products(rows[...], cols, unpermuted[...], z_steps()[1:2], store)
    products(center_rows[...], center_cols, unpermuted[...], z_steps()[2:], lambda i, value: store(i + 3, value))


def far_kernel(keep, first, second, third, out):
    total = keep[...]
    for pair, block in enumerate((first, second, third)):
        total += received(pair, block[...])
    out[...] = total.astype(BF16)


def near_kernel(center, outer, after, first, second, third):
    del after
    for pair, out in enumerate((first, second, third)):
        at = toward(pair)
        out[...] = (center[at] + outer[at // 2].astype(F32)).astype(BF16)


def select_kernel(
    count_ref, skel_hbm, order_hbm, self_hbm, near_middle, after, rows_out, cols_out, chosen_out, self_vmem, extra_out, skel, order, sems
):
    del after
    copies = [
        pltpu.make_async_copy(skel_hbm, skel, sems.at[0]),
        pltpu.make_async_copy(order_hbm, order, sems.at[1]),
        pltpu.make_async_copy(self_hbm, self_vmem, sems.at[2]),
    ]
    for copy in copies:
        copy.start()
    size = self_vmem.shape[0]
    count = count_ref[0]
    points = lax.broadcasted_iota(jnp.int32, (size, size), 0)
    lanes = lax.broadcasted_iota(jnp.int32, (size, size), 1)
    live = (points < count).astype(F32)
    for copy in copies:
        copy.wait()
    rows = (skel[0].astype(F32) * live).astype(BF16)
    cols = (skel[1].astype(F32) * live).astype(BF16)
    hot_t = ((points == order[...]) & (lanes < count)).astype(F32)
    hot = hot_t.T.astype(BF16)
    hot_t = hot_t.astype(BF16)

    def parts(value):
        high = value.astype(BF16)
        rest = value - high.astype(F32)
        middle = rest.astype(BF16)
        return high, middle, (rest - middle.astype(F32)).astype(BF16)

    high, middle, low = parts(self_vmem[...])
    picked = dot(hot, jnp.concatenate([rows, cols, high, middle, low], axis=1))
    rows_out[0:size, :] = rows
    rows_out[size:, :] = picked[:, :size].astype(BF16)
    cols_out[0] = cols
    cols_out[1] = picked[:, size : 2 * size].astype(BF16)
    by_row = (
        picked[:, 2 * size : 3 * size] + picked[:, 3 * size : 4 * size] + picked[:, 4 * size :]
    )
    both = dot(jnp.concatenate(parts(by_row), axis=0), hot_t)
    chosen = both[:size] + both[size : 2 * size] + both[2 * size :]
    chosen_out[...] = chosen
    extra_out[0] = near_middle[...]
    extra_out[1] = chosen.astype(BF16)


def halves(value):
    high = value.astype(BF16)
    return high, (value - high.astype(F32)).astype(BF16)


def change(rows, total, cols):
    high, low = total[0], total[1]
    left_high, left_low = halves(dot(rows, high) + dot(rows, low))
    return dot_t(left_high, cols) + dot_t(left_low, cols)


def child_kernel(center, extra, first, second, third, far, rows, cols, chosen, total, child, child_sent):
    size = chosen.shape[0]
    value = center[1] + extra[0].astype(F32)
    for pair, block in enumerate((first, second, third)):
        value += received(pair, block[...])
    high, low = halves(value + far[...].astype(F32))
    total[0] = high
    total[1] = low
    less = change(rows[size:, :], total, cols[1])
    child[...] = chosen[...] - less
    child_sent[...] = (less - (chosen[...] - chosen[...].astype(BF16).astype(F32))).astype(BF16)


def update_kernel(owner, total, rows, cols, own_self, child, updated_hbm, parent_hbm, updated, mine, sems):
    size = own_self.shape[0]
    zpos = lax.axis_index("bz")
    parity = lax.rem(zpos, 2)
    mine[...] = child[...] * (owner[0, 0, lax.div(zpos, 2)] == parity).astype(F32)
    first = pltpu.make_async_copy(mine, parent_hbm.at[parity], sems.at[0])
    first.start()
    updated[...] = own_self[...] - change(rows[0:size, :], total, cols[0])
    second = pltpu.make_async_copy(updated, updated_hbm, sems.at[1])
    second.start()
    first.wait()
    second.wait()


def on_device(
    skel_blocks,
    row_couple,
    col_couple,
    inverse_rr,
    pivots,
    self_block,
    skel_count,
    skel_order,
    owner_flag,
):
    size = inverse_rr.shape[-1]
    block = (size, size)
    row_couple = row_couple.reshape(3, 3, 3, size, size)
    col_couple = col_couple.reshape(3, 3, 3, size, size)
    inverse = inverse_rr.reshape(block)
    pivots = pivots.reshape(1, size)

    far_other, far_own, other_rows, other_cols, own_rows, own_cols, unpermuted = call(
        first_kernel,
        [(row_couple, "hbm"), (col_couple, "hbm"), (inverse, "hbm"), (pivots, "hbm")],
        [
            pltpu.VMEM((3, *block), BF16),
            pltpu.VMEM((3, *block), F32),
            pltpu.VMEM((6, *block), BF16),
            pltpu.VMEM((6, *block), BF16),
            pltpu.VMEM((3, *block), BF16),
            pltpu.VMEM((3, *block), BF16),
            pltpu.VMEM(block, BF16),
        ],
        [
            pltpu.VMEM((6, *block), BF16),
            pltpu.VMEM((6, *block), BF16),
            pltpu.VMEM(block, BF16),
            pltpu.VMEM((1, size), jnp.int32),
            pltpu.SemaphoreType.DMA((2, 7)),
        ],
    )
    far_other = swap_x(far_other)
    near_other, center_rows, center_cols = call(
        near_other_kernel,
        [
            (row_couple, "hbm"),
            (col_couple, "hbm"),
            (other_rows, "vmem"),
            (other_cols, "vmem"),
            (unpermuted, "vmem"),
        ],
        [pltpu.VMEM((6, *block), BF16), pltpu.VMEM((3, *block), BF16), pltpu.VMEM((3, *block), BF16)],
        [pltpu.SemaphoreType.DMA((2, 1))],
    )
    near_other = swap_x(near_other)
    *far_sides, far_keep = call(
        far_join_kernel,
        [(far_own, "vmem"), (far_other, "vmem")],
        [pltpu.VMEM(block, BF16)] * 3 + [pltpu.VMEM(block, F32)],
        hint=HINT,
    )
    far_sides = swap_y(far_sides)
    outer, middle, center = call(
        near_join_kernel,
        [
            (own_rows, "vmem"),
            (own_cols, "vmem"),
            (center_rows, "vmem"),
            (center_cols, "vmem"),
            (unpermuted, "vmem"),
            (near_other, "vmem"),
            (far_keep, "vmem"),
        ],
        [pltpu.VMEM((2, *block), BF16), pltpu.VMEM(block, BF16), pltpu.VMEM((3, *block), F32)],
    )
    outer = swap_even(outer, "bz")
    (far,) = call(
        far_kernel,
        [(far_keep, "vmem")] + [(side, "vmem") for side in far_sides],
        [pltpu.VMEM(block, BF16)],
        hint=HINT,
    )
    far_sent = far
    far = swap_odd(far, "bz")

    rows, cols, chosen, own_self, extra = call(
        select_kernel,
        [
            (skel_count.reshape(1), "smem"),
            (skel_blocks.reshape(2, size, size), "hbm"),
            (skel_order.reshape(1, size), "hbm"),
            (self_block.reshape(block), "hbm"),
            (middle, "vmem"),
            (far_sent, "vmem"),
        ],
        [
            pltpu.VMEM((2 * size, size), BF16),
            pltpu.VMEM((2, size, size), BF16),
            pltpu.VMEM(block, F32),
            pltpu.VMEM(block, F32),
            pltpu.VMEM((2, *block), BF16),
        ],
        [
            pltpu.VMEM((2, size, size), BF16),
            pltpu.VMEM((1, size), jnp.int32),
            pltpu.SemaphoreType.DMA((3,)),
        ],
    )
    extra = swap_even(extra, "bz")
    near_sides = call(
        near_kernel,
        [(center, "vmem"), (outer, "vmem"), (chosen, "vmem")],
        [pltpu.VMEM(block, BF16)] * 3,
        hint=HINT,
    )
    near_sides = swap_y(near_sides)

    total, child, child_sent = call(
        child_kernel,
        [
            (center, "vmem"),
            (extra, "vmem"),
            *[(side, "vmem") for side in near_sides],
            (far, "vmem"),
            (rows, "vmem"),
            (cols, "vmem"),
            (chosen, "vmem"),
        ],
        [pltpu.VMEM((2, *block), BF16), pltpu.VMEM(block, F32), pltpu.VMEM(block, BF16)],
    )
    partner = swap_even(child_sent, "bz")
    updated, parent = call(
        update_kernel,
        [
            (owner_flag, "smem"),
            (total, "vmem"),
            (rows, "vmem"),
            (cols, "vmem"),
            (own_self, "vmem"),
            (child, "vmem"),
        ],
        [jax.ShapeDtypeStruct(block, F32), jax.ShapeDtypeStruct((2, *block), F32)],
        [pltpu.VMEM(block, F32), pltpu.VMEM(block, F32), pltpu.SemaphoreType.DMA((2,))],
    )
    zpos = lax.axis_index("bz")
    parity = zpos % 2
    flag = lax.dynamic_index_in_dim(owner_flag[0, 0], zpos // 2, 0, keepdims=False)
    theirs = extra[1].astype(F32) - partner.astype(F32)
    theirs = jnp.where(parity == flag, theirs, F32(0.0))
    parent = lax.dynamic_update_index_in_dim(parent, theirs, 1 - parity, 0)
    return (updated[None, None, None], parent[None, None, None])


def solution(mesh):
    in_specs = (
        P("bx", "by", "bz", None, None, None),
        P("bx", "by", "bz", None, None, None),
        P("bx", "by", "bz", None, None, None),
        P("bx", "by", "bz", None, None),
        P("bx", "by", "bz", None),
        P("bx", "by", "bz", None, None),
        P("bx", "by", "bz"),
        P("bx", "by", "bz", None),
        P("bx", "by", None),
    )
    out_specs = (P("bx", "by", "bz", None, None), P("bx", "by", "bz", None, None, None))
    return jax.shard_map(
        on_device, mesh=mesh, in_specs=in_specs, out_specs=out_specs, check_vma=False
    )
```

time: 41.1 us -> 34.8 us (0.85)
  starting transfers between devices: 17.7 us -> 12.2 us
  waiting for transfers between devices: 12 us -> 10.3 us
  Pallas kernels: 9.72 us -> 8.67 us
  other arithmetic: 0 us -> 0.75 us
  between operations: 1.43 us -> 2.11 us
  local copies, waits for them, and re-layouts: 0.01 us -> 0.59 us
    ppermute x9 -> x12, starting transfers between devices: 17.7 us -> 12.2 us  [the longest x1 6.02 us: swap_odd(): return lax.ppermute(block, ('bx', axis), route)]
    ppermute x9 -> x12, waiting for transfers between devices: 12 us -> 10.3 us  [the longest x1 6.65 us: swap_odd(): return lax.ppermute(block, ('bx', axis), route)]
    pallas_call x11 -> x9, Pallas kernels: 9.72 us -> 8.67 us  [call(): pl.pallas_call(kernel, out_shape=tuple(outputs), in_specs=[pl.BlockSpec(m...]
    dynamic_update_slice x0 -> x1, other arithmetic: none -> 0.75 us  [on_device(): parent = lax.dynamic_update_index_in_dim(parent, theirs, 1 - parity, 0)]
    dynamic_slice x0 -> x1, local copies, waits for them, and re-layouts: none -> 0.59 us  [on_device(): lax.dynamic_index_in_dim(owner_flag[0, 0], zpos // 2, 0, keepdims=False)]
  transfers between devices with their start and end apart: 9 -> 12, of which waited for: 4 -> 4; matrix products, arithmetic and copies ran while one was open for 0% -> 2% of each run, Pallas kernels for 11% -> 17%
where the time goes in v2:
time: 34.8 us; the launch traced here: 34.6 us
  starting transfers between devices  12.2 us (35%)
  waiting for transfers between devices  10.3 us (30%)
  Pallas kernels  8.67 us (25%)
  between operations  2.11 us (6%)
  other arithmetic  0.75 us (2%)
  local copies, waits for them, and re-layouts  0.59 us (2%)
    pallas_call x9, Pallas kernels, call(): pl.pallas_call(kernel, out_shape=tuple(outputs), in_specs=[pl.BlockSpec(m...  8.67 us
    ppermute x1, waiting for transfers between devices, swap_odd(): return lax.ppermute(block, ('bx', axis), route)  6.65 us
    ppermute x1, starting transfers between devices, swap_odd(): return lax.ppermute(block, ('bx', axis), route)  6.02 us
    ppermute x6, starting transfers between devices, swap_y(): out.append(lax.ppermute(block, ('bx', 'by'), route))  4.43 us
    ppermute x3, waiting for transfers between devices, swap_even(): return lax.ppermute(block, axis, route)  1.94 us
    ppermute x6, waiting for transfers between devices, swap_y(): out.append(lax.ppermute(block, ('bx', 'by'), route))  1.65 us
    ppermute x3, starting transfers between devices, swap_even(): return lax.ppermute(block, axis, route)  1.12 us
    dynamic_update_slice x1, other arithmetic, on_device(): parent = lax.dynamic_update_index_in_dim(parent, theirs, 1 - parity, 0)  0.75 us
  transfers between devices with their start and end apart: 12, of which 4 were waited for; matrix products, arithmetic and copies ran while one was open for 2% of the time, Pallas kernels for 17%

profile of v2, /device:TPU:62, one launch (start us, length us, event | category | flops | bytes accessed | tf_op | source)
XLA Modules:
  0.0 34.6 jit_solution(787148932118838477)
XLA Ops:
  0.6 2.3 %shard_map.104 = (bf16[3,256,256]{2,1,0:T(8,128)(2,1)S(1)}, f32[3,256,256]{2,1,0:T(8,128)S(1)}, bf16[6,256,256]{2,1,0:T(8,128)(2,1)S(1)}, bf16[6,256,256]{2,1,0:...) custom-call(bf16[3,3,3,256,256]{4,3,2,1,0:T(8,128)(2,1)} %bitcast.21, ...), custom_call_target="tpu_custom_call" | custom-call | tf_op jit(solution)/shard_map/pallas_call | solution.py:94
  2.9 0.1 collective-permute-start.1
  3.0 1.3 %shard_map.105 = (bf16[6,256,256]{2,1,0:T(8,128)(2,1)S(1)}, bf16[3,256,256]{2,1,0:T(8,128)(2,1)S(1)}, bf16[3,256,256]{2,1,0:T(8,128)(2,1)S(1)}) custom-call(bf16[3,3,3,256,256]{4,3,2,1,0:T(8,128)(2,1)} %bitcast.22, bf16[3,3,3,256,256]{4,3,2,1,0:T(8,128)(2,1)} %bitcast.24, bf16[6,256,256]{2,1,0:T(8,128)(2,1)S(1)} %get-tuple-element.34.rows, ...), custom_call_target="tpu_custom_call" | custom-call | tf_op jit(solution)/shard_map/pallas_call | solution.py:94
  4.3 0.6 %collective-permute-start = (bf16[6,256,256]{2,1,0:T(8,128)(2,1)S(1)}, bf16[6,256,256]{2,1,0:T(8,128)(2,1)S(1)}, u32[]{:S(2)}, u32[]{:S(2)}) collective-permute-start(bf16[6,256,256]{2,1,0:T(8,128)(2,1)S(1)} %get-tuple-element.39), channel_id=1, source_target_pairs={{0,128},{128,0},{1,129},{129,1},{2,130},{130,2},{3,131},{131,3},{4... | collective-permute-start | bytes 2359304 | tf_op jit(solution)/shard_map/ppermute | solution.py:17
  5.0 0.2 collective-permute-start.2
  5.2 1.9 %collective-permute-start.3 = (bf16[256,256]{1,0:T(8,128)(2,1)S(1)}, bf16[256,256]{1,0:T(8,128)(2,1)S(1)}, u32[]{:S(2)}, u32[]{:S(2)}) collective-permute-start(bf16[256,256]{1,0:T(8,128)(2,1)S(1)} %get-tuple-element.46), channel_id=1, source_target_pairs={{0,128},{32,64},{64,32},{96,224},{128,0},{160,192},{192,160},{224,... | collective-permute-start | bytes 393224 | tf_op jit(solution)/shard_map/ppermute | solution.py:53
  7.1 0.1 collective-permute-start.4
  7.9 0.7 %shard_map.107 = (bf16[2,256,256]{2,1,0:T(8,128)(2,1)S(1)}, bf16[256,256]{1,0:T(8,128)(2,1)S(1)}, f32[3,256,256]{2,1,0:T(8,128)S(1)}) custom-call(bf16[3,256,256]{2,1,0:T(8,128)(2,1)S(1)} %get-tuple-element.32.rows, bf16[3,256,256]{2,1,0:T(8,128)(2,1)S(1)} %get-tuple-element.33.cols, bf16[3,256,256]{2,1,0:T(8,128)(2,1)S(1)} %get-tuple-element.37.center_rows, ...), custom_call_target="tpu_custom_call" | custom-call | tf_op jit(solution)/shard_map/pallas_call | solution.py:94
  8.6 0.9 %collective-permute-start.6 = (bf16[2,256,256]{2,1,0:T(8,128)(2,1)S(1)}, bf16[2,256,256]{2,1,0:T(8,128)(2,1)S(1)}, u32[]{:S(2)}, u32[]{:S(2)}) collective-permute-start(bf16[2,256,256]{2,1,0:T(8,128)(2,1)S(1)} %get-tuple-element.49), channel_id=1, source_target_pairs={{0,1},{1,0},{2,3},{3,2},{4,5},{5,4},{6,7},{7,6},{8,9},{9,8},{10,11... | collective-permute-start | bytes 786440 | tf_op jit(solution)/shard_map/ppermute | solution.py:24
  9.5 1.0 %collective-permute-done.2.first = bf16[256,256]{1,0:T(8,128)(2,1)S(1)} collective-permute-done((bf16[256,256]{1,0:T(8,128)(2,1)S(1)}, bf16[256,256]{1,0:T(8,128)(2,1)S(1)}, u32[]{:S(2)}, u32[]{:S(2)}) %collective-permute-start.2) | collective-permute-done | bytes 131104 | tf_op jit(solution)/shard_map/ppermute | solution.py:53
  10.5 0.7 %collective-permute-done.3.second = bf16[256,256]{1,0:T(8,128)(2,1)S(1)} collective-permute-done((bf16[256,256]{1,0:T(8,128)(2,1)S(1)}, bf16[256,256]{1,0:T(8,128)(2,1)S(1)}, u32[]{:S(2)}, u32[]{:S(2)}) %collective-permute-start.3) | collective-permute-done | bytes 131104 | tf_op jit(solution)/shard_map/ppermute | solution.py:53
  11.2 0.1 shard_map.108.after
  11.3 6.0 %collective-permute-start.10 = (bf16[256,256]{1,0:T(8,128)(2,1)S(1)}, bf16[256,256]{1,0:T(8,128)(2,1)S(1)}, u32[]{:S(2)}, u32[]{:S(2)}) collective-permute-start(bf16[256,256]{1,0:T(8,128)(2,1)S(1)} %shard_map.108.after), channel_id=1, source_target_pairs={{1,2},{2,1},{3,4},{4,3},{5,6},{6,5},{7,8},{8,7},{9,10},{10,9},{11,... | collective-permute-start | bytes 393224 | tf_op jit(solution)/shard_map/ppermute | solution.py:36
  17.3 1.8 %shard_map.109 = (bf16[512,256]{1,0:T(8,128)(2,1)S(1)}, bf16[2,256,256]{2,1,0:T(8,128)(2,1)S(1)}, f32[256,256]{1,0:T(8,128)S(1)}, f32[256,256]{1,0:T(8,128)S(1)}, bf16[2,256,256]{2,1,0:T(8,128)(2,1)S(1)}) custom-call(s32[1]{0:T(128)} %bitcast.20.count_ref, bf16[2,256,256]{2,1,0:T(8,128)(2,1)} %bitcast.25, s32[1,256]{1,0:T(1,128)} %bitcast.28, ...), custom_call_target="tpu_custom_call" | custom-call | tf_op jit(solution)/shard_map/pallas_call | solution.py:94
  19.1 0.1 collective-permute-start.5
  19.4 0.4 %collective-permute-start.7 = (bf16[256,256]{1,0:T(8,128)(2,1)S(1)}, bf16[256,256]{1,0:T(8,128)(2,1)S(1)}, u32[]{:S(2)}, u32[]{:S(2)}) collective-permute-start(bf16[256,256]{1,0:T(8,128)(2,1)S(1)} %get-tuple-element.51), channel_id=1, source_target_pairs={{0,32},{32,0},{64,192},{96,224},{128,160},{160,128},{192,64},{224,... | collective-permute-start | bytes 393224 | tf_op jit(solution)/shard_map/ppermute | solution.py:53
  19.7 1.7 %collective-permute-start.8 = (bf16[256,256]{1,0:T(8,128)(2,1)S(1)}, bf16[256,256]{1,0:T(8,128)(2,1)S(1)}, u32[]{:S(2)}, u32[]{:S(2)}) collective-permute-start(bf16[256,256]{1,0:T(8,128)(2,1)S(1)} %get-tuple-element.52), channel_id=1, source_target_pairs={{0,128},{32,64},{64,32},{96,224},{128,0},{160,192},{192,160},{224,... | collective-permute-start | bytes 393224 | tf_op jit(solution)/shard_map/ppermute | solution.py:53
  21.4 0.1 collective-permute-start.9
  21.5 6.7 %collective-permute-done.10.far = bf16[256,256]{1,0:T(8,128)(2,1)S(1)} collective-permute-done((bf16[256,256]{1,0:T(8,128)(2,1)S(1)}, bf16[256,256]{1,0:T(8,128)(2,1)S(1)}, u32[]{:S(2)}, u32[]{:S(2)}) %collective-permute-start.10) | collective-permute-done | bytes 131104 | tf_op jit(solution)/shard_map/ppermute | solution.py:36
  28.2 0.6 %shard_map.111 = (bf16[2,256,256]{2,1,0:T(8,128)(2,1)S(1)}, f32[256,256]{1,0:T(8,128)S(1)}, bf16[256,256]{1,0:T(8,128)(2,1)S(1)}) custom-call(f32[3,256,256]{2,1,0:T(8,128)S(1)} %get-tuple-element.43.center, bf16[2,256,256]{2,1,0:T(8,128)(2,1)S(1)} %collective-permute-done.5.extra, bf16[256,256]{1,0:T(8,128)(2,1)S(1)} %collective-permute-done.7.first, ...), custom_call_target="tpu_custom_call" | custom-call | tf_op jit(solution)/shard_map/pallas_call | solution.py:94
  28.9 0.6 %constant_dynamic-slice_fusion = s32[1,1,1]{2,1,0:T(1,128)} fusion(s32[1,1,16]{2,1,0:T(1,128)S(1)} %copy-done, s32[]{:T(128)S(6)} %select_n.29), kind=kLoop, calls=%fused_computation.5 | loop fusion | bytes 12 | tf_op jit(solution)/shard_map/jit(dynamic_index_in_dim)/dynamic_slice | solution.py:449
  30.2 1.7 %shard_map.112 = (f32[256,256]{1,0:T(8,128)}, f32[2,256,256]{2,1,0:T(8,128)}) custom-call(s32[1,1,16]{2,1,0:T(1,128)S(1)} %copy-done, bf16[2,256,256]{2,1,0:T(8,128)(2,1)S(1)} %get-tuple-element.56.total, bf16[512,256]{1,0:T(8,128)(2,1)S(1)} %get-tuple-element.54.rows, bf16[2,256,256]{2,1,0:T(8,128)(2,1)S(1)} %get-tuple-element.55.cols, ...), custom_call_target="tpu_custom_call" | custom-call | tf_op jit(solution)/shard_map/pallas_call | solution.py:94
  31.9 1.9 %collective-permute-done.11 = bf16[256,256]{1,0:T(8,128)(2,1)S(1)} collective-permute-done((bf16[256,256]{1,0:T(8,128)(2,1)S(1)}, bf16[256,256]{1,0:T(8,128)(2,1)S(1)}, u32[]{:S(2)}, u32[]{:S(2)}) %collective-permute-start.11) | collective-permute-done | bytes 131104 | tf_op jit(solution)/shard_map/ppermute | solution.py:24
  33.9 0.7 %fusion.2 = f32[1,1,1,2,256,256]{5,4,3,2,1,0:T(8,128)} fusion(f32[1,1,1,2,256,256]{5,4,3,2,1,0:T(8,128)} %bitcast.30, s32[]{:T(128)S(6)} %select_n.32, bf16[256,256]{1,0:T(8,128)(2,1)S(1)} %collective-permute-done.11, bf16[2,256,256]{2,1,0:T(8,128)(2,1)S(1)} %collective-permute-done.5.extra, pred[]{:T(512)S(6)} %eq.5), kind=kLoop, calls=%fused_computation.3 | loop fusion | flops 262144 | bytes 524293 | tf_op jit(solution)/shard_map/jit(dynamic_update_index_in_dim)/dynamic_update_slice | solution.py:452
  (13 shorter events, 0.3 us)
Async XLA Ops:
  2.9 2.0 %collective-permute-start.1 = (bf16[3,256,256]{2,1,0:T(8,128)(2,1)S(1)}, bf16[3,256,256]{2,1,0:T(8,128)(2,1)S(1)}, u32[]{:S(2)}, u32[]{:S(2)}) collective-permute-start(bf16[3,256,256]{2,1,0:T(8,128)(2,1)S(1)} %get-tuple-element.41), channel_id=1, source_target_pairs={{0,128},{128,0},{1,129},{129,1},{2,130},{130,2},{3,131},{131,3},{4... | collective-permute-start | bytes 1179656 | tf_op jit(solution)/shard_map/ppermute | solution.py:17
  4.3 3.6 %collective-permute-start = (bf16[6,256,256]{2,1,0:T(8,128)(2,1)S(1)}, bf16[6,256,256]{2,1,0:T(8,128)(2,1)S(1)}, u32[]{:S(2)}, u32[]{:S(2)}) collective-permute-start(bf16[6,256,256]{2,1,0:T(8,128)(2,1)S(1)} %get-tuple-element.39), channel_id=1, source_target_pairs={{0,128},{128,0},{1,129},{129,1},{2,130},{130,2},{3,131},{131,3},{4... | collective-permute-start | bytes 2359304 | tf_op jit(solution)/shard_map/ppermute | solution.py:17
  5.0 5.5 %collective-permute-start.2 = (bf16[256,256]{1,0:T(8,128)(2,1)S(1)}, bf16[256,256]{1,0:T(8,128)(2,1)S(1)}, u32[]{:S(2)}, u32[]{:S(2)}) collective-permute-start(bf16[256,256]{1,0:T(8,128)(2,1)S(1)} %get-tuple-element.45), channel_id=1, source_target_pairs={{0,32},{32,0},{64,192},{96,224},{128,160},{160,128},{192,64},{224,... | collective-permute-start | bytes 393224 | tf_op jit(solution)/shard_map/ppermute | solution.py:53
  5.2 6.0 %collective-permute-start.3 = (bf16[256,256]{1,0:T(8,128)(2,1)S(1)}, bf16[256,256]{1,0:T(8,128)(2,1)S(1)}, u32[]{:S(2)}, u32[]{:S(2)}) collective-permute-start(bf16[256,256]{1,0:T(8,128)(2,1)S(1)} %get-tuple-element.46), channel_id=1, source_target_pairs={{0,128},{32,64},{64,32},{96,224},{128,0},{160,192},{192,160},{224,... | collective-permute-start | bytes 393224 | tf_op jit(solution)/shard_map/ppermute | solution.py:53
  7.1 4.1 %collective-permute-start.4 = (bf16[256,256]{1,0:T(8,128)(2,1)S(1)}, bf16[256,256]{1,0:T(8,128)(2,1)S(1)}, u32[]{:S(2)}, u32[]{:S(2)}) collective-permute-start(bf16[256,256]{1,0:T(8,128)(2,1)S(1)} %get-tuple-element.47), channel_id=1, source_target_pairs={{0,128},{32,160},{64,96},{96,64},{128,0},{160,32},{192,224},{224,1... | collective-permute-start | bytes 393224 | tf_op jit(solution)/shard_map/ppermute | solution.py:53
  8.6 10.6 %collective-permute-start.6 = (bf16[2,256,256]{2,1,0:T(8,128)(2,1)S(1)}, bf16[2,256,256]{2,1,0:T(8,128)(2,1)S(1)}, u32[]{:S(2)}, u32[]{:S(2)}) collective-permute-start(bf16[2,256,256]{2,1,0:T(8,128)(2,1)S(1)} %get-tuple-element.49), channel_id=1, source_target_pairs={{0,1},{1,0},{2,3},{3,2},{4,5},{5,4},{6,7},{7,6},{8,9},{9,8},{10,11... | collective-permute-start | bytes 786440 | tf_op jit(solution)/shard_map/ppermute | solution.py:24
  11.3 16.9 %collective-permute-start.10 = (bf16[256,256]{1,0:T(8,128)(2,1)S(1)}, bf16[256,256]{1,0:T(8,128)(2,1)S(1)}, u32[]{:S(2)}, u32[]{:S(2)}) collective-permute-start(bf16[256,256]{1,0:T(8,128)(2,1)S(1)} %shard_map.108.after), channel_id=1, source_target_pairs={{1,2},{2,1},{3,4},{4,3},{5,6},{6,5},{7,8},{8,7},{9,10},{10,9},{11,... | collective-permute-start | bytes 393224 | tf_op jit(solution)/shard_map/ppermute | solution.py:36
  19.1 9.1 %collective-permute-start.5 = (bf16[2,256,256]{2,1,0:T(8,128)(2,1)S(1)}, bf16[2,256,256]{2,1,0:T(8,128)(2,1)S(1)}, u32[]{:S(2)}, u32[]{:S(2)}) collective-permute-start(bf16[2,256,256]{2,1,0:T(8,128)(2,1)S(1)} %get-tuple-element.48), channel_id=1, source_target_pairs={{0,1},{1,0},{2,3},{3,2},{4,5},{5,4},{6,7},{7,6},{8,9},{9,8},{10,11... | collective-permute-start | bytes 786440 | tf_op jit(solution)/shard_map/ppermute | solution.py:24
  19.3 9.7 %copy-start = (s32[1,1,16]{2,1,0:T(1,128)S(1)}, s32[1,1,16]{2,1,0:T(1,128)}, u32[]{:S(2)}) copy-start(s32[1,1,16]{2,1,0:T(1,128)} %owner.1) | copy-start | bytes 196
  19.4 8.8 %collective-permute-start.7 = (bf16[256,256]{1,0:T(8,128)(2,1)S(1)}, bf16[256,256]{1,0:T(8,128)(2,1)S(1)}, u32[]{:S(2)}, u32[]{:S(2)}) collective-permute-start(bf16[256,256]{1,0:T(8,128)(2,1)S(1)} %get-tuple-element.51), channel_id=1, source_target_pairs={{0,32},{32,0},{64,192},{96,224},{128,160},{160,128},{192,64},{224,... | collective-permute-start | bytes 393224 | tf_op jit(solution)/shard_map/ppermute | solution.py:53
  19.7 8.5 %collective-permute-start.8 = (bf16[256,256]{1,0:T(8,128)(2,1)S(1)}, bf16[256,256]{1,0:T(8,128)(2,1)S(1)}, u32[]{:S(2)}, u32[]{:S(2)}) collective-permute-start(bf16[256,256]{1,0:T(8,128)(2,1)S(1)} %get-tuple-element.52), channel_id=1, source_target_pairs={{0,128},{32,64},{64,32},{96,224},{128,0},{160,192},{192,160},{224,... | collective-permute-start | bytes 393224 | tf_op jit(solution)/shard_map/ppermute | solution.py:53
  21.4 6.8 %collective-permute-start.9 = (bf16[256,256]{1,0:T(8,128)(2,1)S(1)}, bf16[256,256]{1,0:T(8,128)(2,1)S(1)}, u32[]{:S(2)}, u32[]{:S(2)}) collective-permute-start(bf16[256,256]{1,0:T(8,128)(2,1)S(1)} %get-tuple-element.53), channel_id=1, source_target_pairs={{0,128},{32,160},{64,96},{96,64},{128,0},{160,32},{192,224},{224,1... | collective-permute-start | bytes 393224 | tf_op jit(solution)/shard_map/ppermute | solution.py:53
  28.8 5.1 %collective-permute-start.11 = (bf16[256,256]{1,0:T(8,128)(2,1)S(1)}, bf16[256,256]{1,0:T(8,128)(2,1)S(1)}, u32[]{:S(2)}, u32[]{:S(2)}) collective-permute-start(bf16[256,256]{1,0:T(8,128)(2,1)S(1)} %get-tuple-element.61), channel_id=1, source_target_pairs={{0,1},{1,0},{2,3},{3,2},{4,5},{5,4},{6,7},{7,6},{8,9},{9,8},{10,11... | collective-permute-start | bytes 393224 | tf_op jit(solution)/shard_map/ppermute | solution.py:24
